TPU v7x, 32 devices: a whole 2x2x4 slice. The times are simulated.
32 devices in a mesh: dp: 4 (over y, x), seq: 4 (over z), dir: 2 (over core).
Axes of the slice: x: 2, y: 2, z: 4, core: 2. Of those that a mesh axis runs over, the one named last changes fastest.
Arguments:
- tokens: bfloat16 [8, 1280, 768], P('dp', ('seq', 'dir')), may hold values from -6 to 6
- starts: int32 [8, 4], P('dp'), may hold values from 0 to 1279, as said below
- pad_len: int32 [8], P('dp'), may hold values from 0 to 160
- norm_gain: float32 [768], replicated, may hold values from 0.5 to 1.5
- w_in: bfloat16 [768, 3328], P(('dp', 'seq', 'dir')), may hold values from -0.21875 to 0.21875
- w_dt: bfloat16 [768, 48], P(('dp', 'seq', 'dir')), may hold values from -0.21875 to 0.21875
- conv_w: float32 [4, 1792], replicated, may hold values from -3 to 3
- conv_b: float32 [1792], replicated, may hold values from -1 to 1
- dt_bias: float32 [48], replicated, may hold values from -4 to 0
- a_log: float32 [48], replicated, may hold values from -5 to -1
- skip: float32 [24], replicated, may hold values from 0.5 to 1.5
- gate_gain: float32 [1536], replicated, may hold values from 0.5 to 1.5
- w_out: bfloat16 [768, 1536], P(('dp', 'seq', 'dir')), may hold values from -0.15625 to 0.15625
- cotangent: bfloat16 [8, 1280, 768], P('dp', ('seq', 'dir')), may hold values from -6 to 6
Outputs:
- mixed: bfloat16 [8, 1280, 768], P('dp', ('seq', 'dir'))
- tokens_grad: bfloat16 [8, 1280, 768], P('dp', ('seq', 'dir'))
- norm_gain_grad: float32 [768], replicated
- w_in_grad: float32 [768, 3328], P(('dp', 'seq', 'dir'))
- w_dt_grad: float32 [768, 48], P(('dp', 'seq', 'dir'))
- conv_w_grad: float32 [4, 1792], replicated
- conv_b_grad: float32 [1792], replicated
- dt_bias_grad: float32 [48], replicated
- a_log_grad: float32 [48], replicated
- skip_grad: float32 [24], replicated
- gate_gain_grad: float32 [1536], replicated
- w_out_grad: float32 [768, 1536], P(('dp', 'seq', 'dir'))
Inputs may be any that keep to these rules, and one draw needn't show every extreme that they name: `starts`: entry 0 of every row is 0; a position is the first token of a sequence where it equals some entry of its row.
All inputs are finite; a program needn't handle non-finite values.
Results may differ from a plain program's by a relative error of at most 0.012.
Values may be sent and summed in bfloat16 or wider, within the bound.
A program may use at most 128 MiB of HBM per device.

v0:
```python
import functools

import jax
import jax.numpy as jnp
from jax import lax
from jax.experimental import pallas as pl
from jax.experimental.pallas import tpu as pltpu
from jax.sharding import PartitionSpec as P

BLOCK = 160
HALO = 16
LANES = 128
CARRY = 16
EPSILON = 1e-05
BF = jnp.bfloat16
F32 = jnp.float32
FAR = -1e30
VMEM_BYTES = 58 * 1024 * 1024


def dot(a, b):
    return lax.dot_general(a, b, (((1,), (0,)), ((), ())), preferred_element_type=F32)


def dot_nt(a, b):
    return lax.dot_general(a, b, (((1,), (1,)), ((), ())), preferred_element_type=F32)


def dot_tn(a, b):
    return lax.dot_general(a, b, (((0,), (0,)), ((), ())), preferred_element_type=F32)


def pieces(values, count):
    parts = []
    for _ in range(count - 1):
        part = values.astype(BF)
        parts.append(part)
        values = values - part.astype(F32)
    parts.append(values.astype(BF))
    return parts


def exact(op, values, ones, count):
    total = None
    for part in pieces(values, count):
        term = op(part, ones)
        total = term if total is None else total + term
    return total


def head_map(first, width, head_dim):
    lane = lax.broadcasted_iota(jnp.int32, (LANES, width), 0)
    head = lax.broadcasted_iota(jnp.int32, (LANES, width), 1) // head_dim
    return jnp.where(lane == head + first, 1.0, 0.0).astype(BF)


def head_maps(heads, width, head_dim):
    return head_map(0, width, head_dim), head_map(heads, width, head_dim)


def triangles():
    row = lax.broadcasted_iota(jnp.int32, (BLOCK, BLOCK), 0)
    col = lax.broadcasted_iota(jnp.int32, (BLOCK, BLOCK), 1)
    return (
        jnp.where(row >= col, 1.0, 0.0).astype(BF),
        jnp.where(row <= col, 1.0, 0.0).astype(BF),
    )


def doc_of(places, starts_ref, row):
    total = (starts_ref[row, 0] <= places).astype(jnp.int32)
    for j in range(1, starts_ref.shape[1]):
        total = total + (starts_ref[row, j] <= places).astype(jnp.int32)
    return total


def column_places(count, first):
    return lax.broadcasted_iota(jnp.int32, (count, 1), 0) + first


def front(dims, info, starts, pads, halo, own, other, gain, w_pre, conv_w, conv_b, bias, a_log,
          normed_o, pre_o, xbc_o, dsil_o, tab_o, cumt_o, v_o, local_o, decay_o, send_o, xs, ps):
    heads, head_dim, state, row_len = dims
    width = heads * head_dim
    row = pl.program_id(0)
    base, core = info[0, 0], info[0, 1]
    half = own.shape[1]
    span = 2 * half
    blocks = span // BLOCK
    conv_len = conv_w.shape[0]
    conv_width = conv_w.shape[1]
    xs[0:HALO] = halo[0].astype(F32)
    xs[pl.ds(pl.multiple_of(HALO + core * half, 16), half)] = own[0].astype(F32)
    xs[pl.ds(pl.multiple_of(HALO + (1 - core) * half, 16), half)] = other[0].astype(F32)
    x = xs[...]
    scale = lax.rsqrt(jnp.mean(x * x, axis=-1, keepdims=True) + EPSILON)
    normed = (x * scale * gain[...]).astype(BF)
    normed_o[0] = normed
    projected = dot(normed, w_pre[...])
    pre = projected[:, :conv_width].astype(BF)
    pre_o[0] = pre
    ps[...] = pre.astype(F32)
    raw = projected[HALO:, conv_width:].astype(BF).astype(F32)
    places = column_places(span, base)
    doc = doc_of(places, starts, row)
    valid = (places < row_len - pads[row, 0]).astype(F32)
    summed = conv_b[...]
    for k in range(conv_len):
        back = conv_len - 1 - k
        ok = (doc_of(places - back, starts, row) == doc).astype(F32)
        summed = summed + ps[HALO - back : HALO - back + span] * conv_w[k : k + 1] * ok
    gate = 1.0 / (1.0 + jnp.exp(-summed))
    xbc = (summed * gate * valid).astype(BF)
    xbc_o[0] = xbc
    dsil_o[0] = gate * (1.0 + summed * (1.0 - gate)) * valid
    u = xbc[:, :width].astype(F32)
    map_f, map_b = head_maps(heads, width, head_dim)
    lower, upper = triangles()
    forward = lax.broadcasted_iota(jnp.int32, (1, LANES), 1) < heads
    shifted_raw = raw + bias[...]
    step = jnp.maximum(shifted_raw, 0.0) + jnp.log1p(jnp.exp(-jnp.abs(shifted_raw)))
    slope = 1.0 / (1.0 + jnp.exp(-shifted_raw))
    logs = -step * jnp.exp(a_log[...])
    tab_o[0, 0] = step
    tab_o[0, 4] = slope
    locals_f, locals_b, decays_f, decays_b = [], [], [], []
    for b in range(blocks):
        at = slice(b * BLOCK, (b + 1) * BLOCK)
        step_b, logs_b, doc_b = step[at], logs[at], doc[at]
        cum = jnp.where(
            forward,
            exact(lambda p, m: dot(m, p), logs_b, lower, 3),
            exact(lambda p, m: dot(m, p), logs_b, upper, 3),
        )
        turned = jnp.where(
            lax.broadcasted_iota(jnp.int32, (LANES, 1), 0) < heads,
            exact(lambda p, m: dot_tn(p, m), logs_b, upper, 3),
            exact(lambda p, m: dot_tn(p, m), logs_b, lower, 3),
        )
        cumt_o[0, b] = turned[: cumt_o.shape[2]]
        first_place = base + b * BLOCK
        end_f = doc_of(first_place + BLOCK - 1, starts, row)
        end_b = doc_of(first_place, starts, row)
        near_f = doc_of(first_place - 1, starts, row)
        near_b = doc_of(first_place + BLOCK, starts, row)
        final = jnp.where(forward, cum[BLOCK - 1 : BLOCK], cum[0:1])
        tail = jnp.exp(final - cum) * (
            doc_b == jnp.where(forward, end_f, end_b)
        ).astype(F32)
        reach = jnp.exp(cum) * (doc_b == jnp.where(forward, near_f, near_b)).astype(F32)
        tab_o[0, 1, at] = cum
        tab_o[0, 2, at] = tail
        tab_o[0, 3, at] = reach
        decay = jnp.broadcast_to(
            jnp.where(forward, reach[BLOCK - 1 : BLOCK], reach[0:1]), (8, LANES)
        )
        for d, head_ones, kept, rates in (
            (0, map_f, locals_f, decays_f),
            (1, map_b, locals_b, decays_b),
        ):
            u_b = u[at]
            v_o[0, d, at] = (exact(dot, step_b, head_ones, 2) * u_b).astype(BF)
            tailed = (exact(dot, tail * step_b, head_ones, 2) * u_b).astype(BF)
            b_mat = xbc[at, width + d * state : width + (d + 1) * state]
            local = dot_tn(b_mat, tailed)
            rate = exact(dot, decay, head_ones, 3)
            local_o[0, b, d] = local
            decay_o[0, b, d] = rate
            kept.append(local)
            rates.append(rate[0:1])
    for d, kept, rates, order in (
        (0, locals_f, decays_f, range(blocks)),
        (1, locals_b, decays_b, reversed(range(blocks))),
    ):
        total, rate = None, None
        for b in order:
            total = kept[b] if total is None else rates[b] * total + kept[b]
            rate = rates[b] if rate is None else rate * rates[b]
        send_o[d, 0, 0:state] = total.astype(BF)
        send_o[d, 0, state:] = carried_rows(rate)


def carried_rows(rate):
    coarse = rate.astype(BF)
    fine = (rate - coarse.astype(F32)).astype(BF)
    row = lax.broadcasted_iota(jnp.int32, (CARRY, rate.shape[1]), 0)
    return jnp.where(
        row == 0, coarse.astype(F32), jnp.where(row == 1, fine.astype(F32), 0.0)
    ).astype(BF)


def compose(received, place, count, state, up):
    total, rate = None, None
    for k in range(1, count):
        part = received[(k - 1) if up else (count - k - 1)]
        there = (place - k >= 0) if up else (place + k < count)
        there = there.astype(F32)
        term = part[0:state].astype(F32) * there
        total = term if total is None else total + rate * term
        hop = part[state : state + 1].astype(F32) + part[state + 1 : state + 2].astype(F32)
        rate = hop if rate is None else rate * hop
    return total


def pair_masks(first_place, starts, row):
    rows = lax.broadcasted_iota(jnp.int32, (BLOCK, BLOCK), 0)
    cols = lax.broadcasted_iota(jnp.int32, (BLOCK, BLOCK), 1)
    doc_rows = doc_of(column_places(BLOCK, first_place), starts, row)
    row_places = lax.broadcasted_iota(jnp.int32, (1, BLOCK), 1) + first_place
    same = doc_rows == doc_of(row_places, starts, row)
    return (
        jnp.where(same & (rows > cols), 0.0, FAR),
        jnp.where(same & (rows < cols), 0.0, FAR),
    )


def inner(dims, info, starts, xbc, tab, cumt, v, y_o):
    heads, head_dim, state, _ = dims
    width = heads * head_dim
    row, block = pl.program_id(0), pl.program_id(1)
    masks = pair_masks(info[0, 0] + block * BLOCK, starts, row)
    low_half = lax.broadcasted_iota(jnp.int32, (1, LANES), 1) < head_dim
    for d in range(2):
        b_mat = xbc[0, :, width + d * state : width + (d + 1) * state]
        c_mat = xbc[0, :, width + (2 + d) * state : width + (3 + d) * state]
        scores = dot_nt(c_mat, b_mat)
        for pair in range(heads // 2):
            at = slice(pair * LANES, (pair + 1) * LANES)
            values = v[0, d, :, at]
            outs = []
            for h in (2 * pair, 2 * pair + 1):
                lane = d * heads + h
                gap = tab[0, 0, :, lane : lane + 1] - cumt[0, 0, lane : lane + 1, :]
                mixing = (jnp.exp(gap + masks[d]) * scores).astype(BF)
                outs.append(dot(mixing, values))
            y_o[0, d, :, at] = jnp.where(low_half, outs[0], outs[1])


def outer(dims, count, info, starts, pads, received, local, decay, xbc, tab, y_in, normed, cot_own,
          cot_other, skip, gate_gain, w_gate, w_out, y_o, inc_o, sum_o, z_o, dg_o, dout_o, cs):
    heads, head_dim, state, row_len = dims
    width = heads * head_dim
    row = pl.program_id(0)
    base, core, place = info[0, 0], info[0, 1], info[0, 2]
    half = cot_own.shape[1]
    span = 2 * half
    blocks = span // BLOCK
    parts = [received[k, 0] for k in range(count - 1)]
    entering = [[None] * 2 for _ in range(blocks)]
    now = compose(parts, place, count, state, True)
    for b in range(blocks):
        entering[b][0] = now
        now = decay[0, b, 0, 0:1] * now + local[0, b, 0]
    now = compose(parts, place, count, state, False)
    for b in reversed(range(blocks)):
        entering[b][1] = now
        now = decay[0, b, 1, 0:1] * now + local[0, b, 1]
    maps = head_maps(heads, width, head_dim)
    for b in range(blocks):
        at = slice(b * BLOCK, (b + 1) * BLOCK)
        for d in range(2):
            inc_o[0, b, d] = entering[b][d]
            c_mat = xbc[0, at, width + (2 + d) * state : width + (3 + d) * state]
            raw = dot(c_mat, entering[b][d].astype(BF))
            y_o[0, d, at] = y_in[0, d, at] + exact(dot, tab[0, 0, at], maps[d], 2) * raw
    u = xbc[0, :, :width].astype(F32)
    y = y_o[0, 0] + skip[...] * u + y_o[0, 1]
    z = dot(normed[0, HALO:], w_gate[...])
    v = y * z * (1.0 / (1.0 + jnp.exp(-z)))
    cs[pl.ds(pl.multiple_of(core * half, 16), half)] = cot_own[0].astype(F32)
    cs[pl.ds(pl.multiple_of((1 - core) * half, 16), half)] = cot_other[0].astype(F32)
    places = column_places(span, base)
    valid = (places < row_len - pads[row, 0]).astype(F32)
    d_out = (cs[...] * valid).astype(BF)
    dout_o[0] = d_out
    d_gated = dot(d_out, w_out[...])
    lane = lax.broadcasted_iota(jnp.int32, (1, LANES), 1)
    squares = jnp.sum(v * v, axis=-1, keepdims=True)
    against = jnp.sum(d_gated * gate_gain[...] * v, axis=-1, keepdims=True)
    sum_o[0] = jnp.where(lane == 0, squares, jnp.where(lane == 1, against, 0.0))
    z_o[0] = z
    dg_o[0] = d_gated


def turn(dims, inner_width, sums, others, xbc, tab, y_in, z_in, dg_in, dout, normed, decay, skip,
         gate_gain, w_out, dy_o, dz_o, enter_o, send_o, branch_o, grad_out_o, grad_gate_o, gain_o,
         skip_o, acc_out, acc_gate):
    heads, head_dim, state, _ = dims
    width = heads * head_dim
    row = pl.program_id(0)
    span = dout.shape[1]
    blocks = span // BLOCK
    total = sums[0] + others[0]
    scale = lax.rsqrt(total[:, 0:1] * (1.0 / inner_width) + EPSILON)
    against = total[:, 1:2]
    u = xbc[0, :, :width].astype(F32)
    y = y_in[0, 0] + skip[...] * u + y_in[0, 1]
    z = z_in[0]
    gate = 1.0 / (1.0 + jnp.exp(-z))
    silu = z * gate
    v = y * silu
    unit = v * scale
    gated = (unit * gate_gain[...]).astype(BF)
    d_gated = dg_in[0]
    d_v = scale * (d_gated * gate_gain[...]) - unit * (
        scale * scale * against * (1.0 / inner_width)
    )
    dy = (d_v * silu).astype(BF)
    dz = (d_v * y * gate * (1.0 + z * (1.0 - gate))).astype(BF)
    dy_o[0] = dy
    dz_o[0] = dz
    dy_f = dy.astype(F32)
    branch_o[0] = dot_nt(gated, w_out[...])

    @pl.when(row == 0)
    def _():
        acc_out[...] = jnp.zeros_like(acc_out)
        acc_gate[...] = jnp.zeros_like(acc_gate)
        gain_o[...] = jnp.zeros_like(gain_o)
        skip_o[...] = jnp.zeros_like(skip_o)

    acc_out[...] += dot_tn(dout[0], gated)
    acc_gate[...] += dot_tn(normed[0, HALO:], dz)
    gain_o[...] += jnp.sum(d_gated * unit, axis=0, keepdims=True)
    skip_o[...] += jnp.sum(dy_f * u, axis=0, keepdims=True)

    @pl.when(row == pl.num_programs(0) - 1)
    def _():
        grad_out_o[...] = acc_out[...].astype(BF)
        grad_gate_o[...] = acc_gate[...].astype(BF)

    maps = head_maps(heads, width, head_dim)
    for d in range(2):
        gone, rate = None, None
        for b in reversed(range(blocks)) if d == 0 else range(blocks):
            at = slice(b * BLOCK, (b + 1) * BLOCK)
            c_mat = xbc[0, at, width + (2 + d) * state : width + (3 + d) * state]
            weighed = (exact(dot, tab[0, 0, at], maps[d], 2) * dy_f[at]).astype(BF)
            enter = dot_tn(c_mat, weighed)
            enter_o[0, b, d] = enter
            own = decay[0, b, d, 0:1]
            gone = enter if gone is None else enter + own * gone
            rate = own if rate is None else rate * own
        send_o[d, 0, 0:state] = gone.astype(BF)
        send_o[d, 0, state:] = carried_rows(rate)


def inner_back(dims, info, starts, xbc, tab, cumt, v, dy, y_in, inc, dv_o, dbc_o, along_o):
    heads, head_dim, state, _ = dims
    width = heads * head_dim
    row, block = pl.program_id(0), pl.program_id(1)
    masks = pair_masks(info[0, 0] + block * BLOCK, starts, row)
    low_half = lax.broadcasted_iota(jnp.int32, (1, LANES), 1) < head_dim
    maps = head_maps(heads, width, head_dim)
    dy_all = dy[0].astype(F32)
    along = None
    for d in range(2):
        b_mat = xbc[0, :, width + d * state : width + (d + 1) * state]
        c_mat = xbc[0, :, width + (2 + d) * state : width + (3 + d) * state]
        scores = dot_nt(c_mat, b_mat)
        d_scores = jnp.zeros((BLOCK, BLOCK), F32)
        for pair in range(heads // 2):
            at = slice(pair * LANES, (pair + 1) * LANES)
            values = v[0, d, :, at]
            grads = dy[0, :, at]
            outs = []
            for h in (2 * pair, 2 * pair + 1):
                lane = d * heads + h
                gap = tab[0, 1, :, lane : lane + 1] - cumt[0, 0, lane : lane + 1, :]
                spread = jnp.exp(gap + masks[d])
                mixing = (spread * scores).astype(BF)
                mine = low_half if h % 2 == 0 else ~low_half
                d_mixing = dot_nt(jnp.where(mine, grads, jnp.zeros_like(grads)), values)
                d_scores = d_scores + d_mixing * spread
                outs.append(dot_tn(mixing, grads))
            dv_o[0, d, :, at] = jnp.where(low_half, outs[0], outs[1])
        d_scores = d_scores.astype(BF)
        weighed = (exact(dot, tab[0, 3], maps[d], 2) * dy_all).astype(BF)
        d_c = dot(d_scores, b_mat) + dot_nt(weighed, inc[0, 0, d].astype(BF))
        d_b = dot_tn(d_scores, c_mat)
        dbc_o[0, :, d * state : (d + 1) * state] = d_b
        dbc_o[0, :, (2 + d) * state : (3 + d) * state] = d_c
        term = exact(dot_nt, dy_all * y_in[0, d], maps[d], 2)
        along = term if along is None else along + term
    along_o[0] = along


def back(dims, count, info, starts, received, enter, decay, inc, xbc, tab, v, dv, dbc, along, dy,
         dsil, pre, normed, dz, skip, a_log, conv_w, w_pre, w_gate, grad_pre_o, dn_o, conv_w_o,
         conv_b_o, small_o, acc, pad, ps):
    heads, head_dim, state, _ = dims
    width = heads * head_dim
    row = pl.program_id(0)
    base, place = info[0, 0], info[0, 2]
    span = dy.shape[1]
    blocks = span // BLOCK
    conv_len, conv_width = conv_w.shape
    parts = [received[k, 0] for k in range(count - 1)]
    leaving = [[None] * 2 for _ in range(blocks)]
    now = compose(parts, place, count, state, False)
    for b in reversed(range(blocks)):
        leaving[b][0] = now
        now = enter[0, b, 0] + decay[0, b, 0, 0:1] * now
    now = compose(parts, place, count, state, True)
    for b in range(blocks):
        leaving[b][1] = now
        now = enter[0, b, 1] + decay[0, b, 1, 0:1] * now
    maps = head_maps(heads, width, head_dim)
    lower, upper = triangles()
    forward = lax.broadcasted_iota(jnp.int32, (1, LANES), 1) < heads
    rate = jnp.exp(a_log[...])
    rows = lax.broadcasted_iota(jnp.int32, (BLOCK, 1), 0)

    @pl.when(row == 0)
    def _():
        acc[...] = jnp.zeros_like(acc)
        conv_w_o[...] = jnp.zeros_like(conv_w_o)
        conv_b_o[...] = jnp.zeros_like(conv_b_o)
        small_o[...] = jnp.zeros_like(small_o)
        pad[0:HALO] = jnp.zeros((HALO, conv_width), F32)
        pad[HALO + span :] = jnp.zeros((pad.shape[0] - HALO - span, conv_width), F32)

    raws = []
    for b in range(blocks):
        at = slice(b * BLOCK, (b + 1) * BLOCK)
        u = xbc[0, at, :width].astype(F32)
        step, tail, slope = tab[0, 0, at], tab[0, 2, at], tab[0, 4, at]
        reach = tab[0, 3, at]
        d_u = skip[...] * dy[0, at].astype(F32)
        through = None
        direct = None
        ended = None
        closing = None
        d_bc = []
        for d in range(2):
            leave = leaving[b][d].astype(BF)
            b_mat = xbc[0, at, width + d * state : width + (d + 1) * state]
            v_d = v[0, d, at].astype(F32)
            dv_state = exact(dot, tail, maps[d], 2) * dot(b_mat, leave)
            dv_all = dv[0, d, at] + dv_state
            tailed = (exact(dot, tail * step, maps[d], 2) * u).astype(BF)
            d_bc.append(dot_nt(tailed, leave))
            d_u = d_u + exact(dot, step, maps[d], 2) * dv_all
            terms = (
                exact(dot_nt, v_d * dv_all, maps[d], 2),
                exact(dot_nt, u * dv_all, maps[d], 2),
                exact(
                    dot_nt,
                    jnp.broadcast_to(jnp.sum(v_d * dv_state, axis=0, keepdims=True), (8, width)),
                    maps[d],
                    3,
                ),
                exact(
                    dot_nt,
                    jnp.broadcast_to(
                        jnp.sum(leaving[b][d] * inc[0, b, d], axis=0, keepdims=True), (8, width)
                    ),
                    maps[d],
                    3,
                ),
            )
            if d == 0:
                through, direct, ended, closing = terms
            else:
                through = through + terms[0]
                direct = direct + terms[1]
                ended = ended + terms[2]
                closing = closing + terms[3]
        final = jnp.where(forward, reach[BLOCK - 1 : BLOCK], reach[0:1])
        at_end = jnp.where(
            forward, (rows == BLOCK - 1).astype(F32), (rows == 0).astype(F32)
        )
        d_cum = along[0, at] - through + at_end * (ended[0:1] + closing[0:1] * final)
        d_logs = jnp.where(
            forward,
            exact(lambda p, m: dot(m, p), d_cum, upper, 3),
            exact(lambda p, m: dot(m, p), d_cum, lower, 3),
        )
        d_step = direct - rate * d_logs
        d_raw = d_step * slope
        raws.append(d_raw.astype(BF))
        small_o[0:1] += jnp.sum(d_raw, axis=0, keepdims=True)
        small_o[1:2] += jnp.sum(-step * rate * d_logs, axis=0, keepdims=True)
        pad[HALO + b * BLOCK : HALO + (b + 1) * BLOCK, 0:width] = d_u * dsil[0, at, 0:width]
        d_bc_all = jnp.concatenate(
            [d_bc[0], d_bc[1], jnp.zeros((BLOCK, 2 * state), F32)], axis=1
        )
        pad[HALO + b * BLOCK : HALO + (b + 1) * BLOCK, width:] = (dbc[0, at] + d_bc_all) * dsil[
            0, at, width:
        ]
    ps[...] = pre[0].astype(F32)
    places = column_places(span, base)
    doc = doc_of(places, starts, row)
    outs = pad[HALO : HALO + span]
    conv_b_o[...] += jnp.sum(outs, axis=0, keepdims=True)
    ext_places = column_places(HALO + span, base - HALO)
    ext_doc = doc_of(ext_places, starts, row)
    d_pre = None
    for k in range(conv_len):
        ahead = conv_len - 1 - k
        ok = (doc_of(places - ahead, starts, row) == doc).astype(F32)
        conv_w_o[k : k + 1] += jnp.sum(
            outs * ok * ps[HALO - ahead : HALO - ahead + span], axis=0, keepdims=True
        )
        ok_ext = (doc_of(ext_places + ahead, starts, row) == ext_doc).astype(F32)
        term = pad[ahead : ahead + HALO + span] * ok_ext * conv_w[k : k + 1]
        d_pre = term if d_pre is None else d_pre + term
    d_raws = jnp.concatenate([jnp.zeros((HALO, LANES), BF)] + raws, axis=0)
    d_all = jnp.concatenate([d_pre.astype(BF), d_raws], axis=1)
    acc[...] += dot_tn(normed[0], d_all)
    dn = dot_nt(d_all, w_pre[...])
    dn_o[0, 0:HALO] = dn[0:HALO]
    dn_o[0, HALO:] = dn[HALO:] + dot_nt(dz[0], w_gate[...])

    @pl.when(row == pl.num_programs(0) - 1)
    def _():
        grad_pre_o[...] = acc[...].astype(BF)


def finish(dims, info, pads, own, cot, gain, dn, dn_other, rim_a, rim_b, branch, branch_other,
           mixed_o, grad_o, gain_o, ds):
    row_len = dims[3]
    row = pl.program_id(0)
    base, core, place, count = info[0, 0], info[0, 1], info[0, 2], info[0, 3]
    half = own.shape[1]
    x = own[0].astype(F32)
    places = column_places(half, base + core * half)
    valid = (places < row_len - pads[row, 0]).astype(F32)
    mixed_o[0] = (x + valid * (branch[0] + branch_other[0].astype(F32))).astype(BF)
    ds[...] = dn[0] + dn_other[0].astype(F32)
    takes = ((core == 1) & (place + 1 < count)).astype(F32)
    ds[half - HALO :] += takes * (rim_a[0].astype(F32) + rim_b[0].astype(F32))
    d_normed = ds[...]
    scale = lax.rsqrt(jnp.mean(x * x, axis=-1, keepdims=True) + EPSILON)
    weighed = d_normed * gain[...]
    along = jnp.mean(weighed * x, axis=-1, keepdims=True)
    dx = scale * weighed - x * (scale * scale * scale * along)
    grad_o[0] = (cot[0].astype(F32) + dx).astype(BF)

    @pl.when(row == 0)
    def _():
        gain_o[...] = jnp.zeros_like(gain_o)

    gain_o[...] += jnp.sum(d_normed * x * scale, axis=0, keepdims=True)


SMEM = pl.BlockSpec(memory_space=pltpu.SMEM)


def whole(*shape):
    return pl.BlockSpec(shape, lambda *_: (0,) * len(shape))


def by_row(*shape):
    return pl.BlockSpec((1,) + shape, lambda r, *_: (r,) + (0,) * len(shape))


def second(*shape):
    return pl.BlockSpec(
        (shape[0], 1) + shape[1:], lambda r, *_: (0, r) + (0,) * (len(shape) - 1)
    )


def run(body, grid, ins, outs, scratch=(), flops=0, name=None):
    arrays = [a for a, _ in ins]
    moved = sum(a.size * a.dtype.itemsize for a in arrays) + sum(
        s.size * s.dtype.itemsize for s, _ in outs
    )
    return pl.pallas_call(
        body,
        grid=grid,
        out_shape=[s for s, _ in outs],
        in_specs=[b for _, b in ins],
        out_specs=[b for _, b in outs],
        scratch_shapes=list(scratch),
        compiler_params=pltpu.CompilerParams(
            vmem_limit_bytes=VMEM_BYTES,
            dimension_semantics=("arbitrary",) * len(grid),
        ),
        cost_estimate=pl.CostEstimate(
            flops=flops, bytes_accessed=moved, transcendentals=flops // 500
        ),
        name=name,
    )(*arrays)


def shape_of(dtype, *dims):
    return jax.ShapeDtypeStruct(dims, dtype)


def swapped(value):
    return lax.ppermute(value, "dir", [(0, 1), (1, 0)])


def rotated(value, steps):
    count = lax.axis_size("seq")
    return lax.ppermute(value, "seq", [(i, (i + steps) % count) for i in range(count)])


def rotated_to(value, steps, cross):
    count = lax.axis_size("seq")
    pairs = []
    for i in range(count):
        for c in range(2):
            pairs.append((i * 2 + c, (i + steps) % count * 2 + (1 - c if cross else c)))
    return lax.ppermute(value, ("seq", "dir"), pairs)


def around(value):
    count, place = lax.axis_size("seq"), lax.axis_index("seq")
    out = []
    for k in range(1, count):
        chosen = jnp.where(place + k < count, value[0], value[1])
        out.append(rotated(chosen, k))
    return jnp.stack(out)


def shards(tokens, starts, pad_len, norm_gain, w_in, w_dt, conv_w, conv_b, dt_bias, a_log, skip,
           gate_gain, w_out, cotangent):
    rows, half, model = tokens.shape
    span = 2 * half
    count = lax.axis_size("seq")
    row_len = span * count
    blocks = span // BLOCK
    inner_width = gate_gain.shape[0]
    all_heads = skip.shape[0]
    heads = all_heads // 2
    head_dim = inner_width // all_heads
    width = heads * head_dim
    xbc_width = conv_w.shape[1]
    state = (xbc_width - inner_width) // 4
    conv_len = conv_w.shape[0]
    conv_width = width + 4 * state
    pre_width = conv_width + LANES
    ext = HALO + span
    dims = (heads, head_dim, state, row_len)
    place, core = lax.axis_index("seq"), lax.axis_index("dir")
    info = jnp.stack([place * span, core, place, jnp.int32(count)]).astype(jnp.int32)[None]
    pads = pad_len[:, None]
    shard = w_in.shape[0]
    pad_dt = jnp.zeros((shard, LANES - 2 * heads), BF)

    def columns(c):
        return (
            jnp.concatenate(
                [
                    w_in[:, inner_width + c * width : inner_width + (c + 1) * width],
                    w_in[:, 2 * inner_width :],
                    w_dt[:, c * heads : (c + 1) * heads],
                    w_dt[:, all_heads + c * heads : all_heads + (c + 1) * heads],
                    pad_dt,
                ],
                axis=1,
            ),
            w_in[:, c * width : (c + 1) * width],
            w_out[:, c * width : (c + 1) * width],
        )

    first, latter = columns(0), columns(1)
    is_late = core == 1

    def both(own, other):
        return jnp.where(
            is_late,
            jnp.concatenate([other, own], axis=0),
            jnp.concatenate([own, other], axis=0),
        )

    def gathered(i):
        keep = jnp.where(is_late, latter[i], first[i])
        give = jnp.where(is_late, first[i], latter[i])
        return lax.all_gather(both(keep, swapped(give)), ("dp", "seq"), axis=0, tiled=True)

    w_pre = gathered(0)
    w_gate = gathered(1)
    w_out_c = gathered(2)
    tokens_other = swapped(tokens)
    cot_other = swapped(cotangent)
    rim = tokens[:, half - HALO :]
    halo = jnp.where(is_late, rotated_to(rim, 1, False), rotated_to(rim, 1, True))

    def mine(vector, size):
        return lax.dynamic_slice_in_dim(vector, core * size, size, axis=-1)

    conv_w_c = jnp.concatenate([mine(conv_w[:, :inner_width], width), conv_w[:, inner_width:]], axis=1)
    conv_b_c = jnp.concatenate([mine(conv_b[:inner_width], width), conv_b[inner_width:]])[None]
    filler = jnp.zeros((LANES - 2 * heads,), F32)
    bias_c = jnp.concatenate([mine(dt_bias[:all_heads], heads), mine(dt_bias[all_heads:], heads), filler])[None]
    a_log_c = jnp.concatenate([mine(a_log[:all_heads], heads), mine(a_log[all_heads:], heads), filler])[None]
    skip_c = jnp.repeat(mine(skip, heads), head_dim)[None]
    gate_gain_c = mine(gate_gain, width)[None]
    gain = norm_gain[None]
    packed = 2 * heads + (-2 * heads) % 8
    tokens_all = rows * span
    scan_flops = 4 * tokens_all * BLOCK * LANES * heads

    normed, pre, xbc, dsil, tab, cumt, v, local, decay, send = run(
        functools.partial(front, dims),
        (rows,),
        [
            (info, SMEM), (starts, SMEM), (pads, SMEM),
            (halo, by_row(HALO, model)), (tokens, by_row(half, model)),
            (tokens_other, by_row(half, model)), (gain, whole(1, model)),
            (w_pre, whole(model, pre_width)), (conv_w_c, whole(conv_len, conv_width)),
            (conv_b_c, whole(1, conv_width)), (bias_c, whole(1, LANES)), (a_log_c, whole(1, LANES)),
        ],
        [
            (shape_of(BF, rows, ext, model), by_row(ext, model)),
            (shape_of(BF, rows, ext, conv_width), by_row(ext, conv_width)),
            (shape_of(BF, rows, span, conv_width), by_row(span, conv_width)),
            (shape_of(F32, rows, span, conv_width), by_row(span, conv_width)),
            (shape_of(F32, rows, 5, span, LANES), by_row(5, span, LANES)),
            (shape_of(F32, rows, blocks, packed, BLOCK), by_row(blocks, packed, BLOCK)),
            (shape_of(BF, rows, 2, span, width), by_row(2, span, width)),
            (shape_of(F32, rows, blocks, 2, state, width), by_row(blocks, 2, state, width)),
            (shape_of(F32, rows, blocks, 2, 8, width), by_row(blocks, 2, 8, width)),
            (shape_of(BF, 2, rows, state + CARRY, width), second(2, state + CARRY, width)),
        ],
        [pltpu.VMEM((ext, model), F32), pltpu.VMEM((ext, conv_width), F32)],
        flops=2 * tokens_all * model * pre_width,
        name="front",
    )
    received = around(send)
    at_block = lambda *shape: pl.BlockSpec((1,) + shape, lambda r, b: (r, b) + (0,) * (len(shape) - 1))
    at_second = lambda *shape: pl.BlockSpec((1, shape[0]) + shape[1:], lambda r, b: (r, 0, b, 0))
    block_tab = lambda i: pl.BlockSpec((1, 1, BLOCK, LANES), lambda r, b: (r, i, b, 0))
    (y_inner,) = run(
        functools.partial(inner, dims),
        (rows, blocks),
        [
            (info, SMEM), (starts, SMEM), (xbc, at_block(BLOCK, conv_width)),
            (tab, block_tab(1)), (cumt, at_block(1, packed, BLOCK)),
            (v, at_second(2, BLOCK, width)),
        ],
        [(shape_of(F32, rows, 2, span, width), at_second(2, BLOCK, width))],
        flops=scan_flops,
        name="inner",
    )
    y_both, inc, sums, z, d_gated, d_out = run(
        functools.partial(outer, dims, count),
        (rows,),
        [
            (info, SMEM), (starts, SMEM), (pads, SMEM),
            (received, second(count - 1, state + CARRY, width)),
            (local, by_row(blocks, 2, state, width)), (decay, by_row(blocks, 2, 8, width)),
            (xbc, by_row(span, conv_width)),
            (tab, pl.BlockSpec((1, 1, span, LANES), lambda r: (r, 3, 0, 0))),
            (y_inner, by_row(2, span, width)), (normed, by_row(ext, model)),
            (cotangent, by_row(half, model)), (cot_other, by_row(half, model)),
            (skip_c, whole(1, width)), (gate_gain_c, whole(1, width)),
            (w_gate, whole(model, width)), (w_out_c, whole(model, width)),
        ],
        [
            (shape_of(F32, rows, 2, span, width), by_row(2, span, width)),
            (shape_of(F32, rows, blocks, 2, state, width), by_row(blocks, 2, state, width)),
            (shape_of(F32, rows, span, LANES), by_row(span, LANES)),
            (shape_of(F32, rows, span, width), by_row(span, width)),
            (shape_of(F32, rows, span, width), by_row(span, width)),
            (shape_of(BF, rows, span, model), by_row(span, model)),
        ],
        [pltpu.VMEM((span, model), F32)],
        flops=4 * tokens_all * model * width,
        name="outer",
    )
    sums_other = swapped(sums)
    dy, dz, enter, back_send, branch, grad_out, grad_gate, gate_sum, skip_sum = run(
        functools.partial(turn, dims, inner_width),
        (rows,),
        [
            (sums, by_row(span, LANES)), (sums_other, by_row(span, LANES)),
            (xbc, by_row(span, conv_width)),
            (tab, pl.BlockSpec((1, 1, span, LANES), lambda r: (r, 3, 0, 0))),
            (y_both, by_row(2, span, width)), (z, by_row(span, width)),
            (d_gated, by_row(span, width)), (d_out, by_row(span, model)),
            (normed, by_row(ext, model)), (decay, by_row(blocks, 2, 8, width)),
            (skip_c, whole(1, width)), (gate_gain_c, whole(1, width)),
            (w_out_c, whole(model, width)),
        ],
        [
            (shape_of(BF, rows, span, width), by_row(span, width)),
            (shape_of(BF, rows, span, width), by_row(span, width)),
            (shape_of(F32, rows, blocks, 2, state, width), by_row(blocks, 2, state, width)),
            (shape_of(BF, 2, rows, state + CARRY, width), second(2, state + CARRY, width)),
            (shape_of(F32, rows, span, model), by_row(span, model)),
            (shape_of(BF, model, width), whole(model, width)),
            (shape_of(BF, model, width), whole(model, width)),
            (shape_of(F32, 1, width), whole(1, width)),
            (shape_of(F32, 1, width), whole(1, width)),
        ],
        [pltpu.VMEM((model, width), F32), pltpu.VMEM((model, width), F32)],
        flops=6 * tokens_all * model * width,
        name="turn",
    )
    back_received = around(back_send[::-1])

    def reduced(grad):
        return lax.psum_scatter(grad, ("dp", "seq"), scatter_dimension=0, tiled=True)

    shard_out = reduced(grad_out)
    shard_gate = reduced(grad_gate)
    dv, dbc, along = run(
        functools.partial(inner_back, dims),
        (rows, blocks),
        [
            (info, SMEM), (starts, SMEM), (xbc, at_block(BLOCK, conv_width)),
            (tab, at_second(5, BLOCK, LANES)), (cumt, at_block(1, packed, BLOCK)),
            (v, at_second(2, BLOCK, width)), (dy, at_block(BLOCK, width)),
            (y_both, at_second(2, BLOCK, width)), (inc, at_block(1, 2, state, width)),
        ],
        [
            (shape_of(F32, rows, 2, span, width), at_second(2, BLOCK, width)),
            (shape_of(F32, rows, span, 4 * state), at_block(BLOCK, 4 * state)),
            (shape_of(F32, rows, span, LANES), at_block(BLOCK, LANES)),
        ],
        flops=2 * scan_flops,
        name="inner_back",
    )
    grad_pre, dn, sum_conv_w, sum_conv_b, small = run(
        functools.partial(back, dims, count),
        (rows,),
        [
            (info, SMEM), (starts, SMEM),
            (back_received, second(count - 1, state + CARRY, width)),
            (enter, by_row(blocks, 2, state, width)), (decay, by_row(blocks, 2, 8, width)),
            (inc, by_row(blocks, 2, state, width)), (xbc, by_row(span, conv_width)),
            (tab, by_row(5, span, LANES)), (v, by_row(2, span, width)),
            (dv, by_row(2, span, width)), (dbc, by_row(span, 4 * state)),
            (along, by_row(span, LANES)), (dy, by_row(span, width)),
            (dsil, by_row(span, conv_width)), (pre, by_row(ext, conv_width)),
            (normed, by_row(ext, model)), (dz, by_row(span, width)),
            (skip_c, whole(1, width)), (a_log_c, whole(1, LANES)),
            (conv_w_c, whole(conv_len, conv_width)), (w_pre, whole(model, pre_width)),
            (w_gate, whole(model, width)),
        ],
        [
            (shape_of(BF, model, pre_width), whole(model, pre_width)),
            (shape_of(F32, rows, ext, model), by_row(ext, model)),
            (shape_of(F32, conv_len, conv_width), whole(conv_len, conv_width)),
            (shape_of(F32, 1, conv_width), whole(1, conv_width)),
            (shape_of(F32, 8, LANES), whole(8, LANES)),
        ],
        [
            pltpu.VMEM((model, pre_width), F32),
            pltpu.VMEM((ext + 8, conv_width), F32),
            pltpu.VMEM((ext, conv_width), F32),
        ],
        flops=6 * tokens_all * model * pre_width,
        name="back",
    )
    shard_pre = reduced(grad_pre)

    def halves(values, first_row):
        keep = lax.dynamic_slice_in_dim(values, first_row + core * half, half, axis=1)
        give = lax.dynamic_slice_in_dim(values, first_row + (1 - core) * half, half, axis=1)
        return keep, swapped(give.astype(BF))

    dn_own, dn_other = halves(dn, HALO)
    branch_own, branch_other = halves(branch, 0)
    edge = dn[:, :HALO].astype(BF)
    rim_a, rim_b = rotated_to(edge, -1, False), rotated_to(edge, -1, True)
    mixed, tokens_grad, gain_sum = run(
        functools.partial(finish, dims),
        (rows,),
        [
            (info, SMEM), (pads, SMEM), (tokens, by_row(half, model)),
            (cotangent, by_row(half, model)), (gain, whole(1, model)),
            (dn_own, by_row(half, model)), (dn_other, by_row(half, model)),
            (rim_a, by_row(HALO, model)), (rim_b, by_row(HALO, model)),
            (branch_own, by_row(half, model)), (branch_other, by_row(half, model)),
        ],
        [
            (shape_of(BF, rows, half, model), by_row(half, model)),
            (shape_of(BF, rows, half, model), by_row(half, model)),
            (shape_of(F32, 1, model), whole(1, model)),
        ],
        [pltpu.VMEM((half, model), F32)],
        name="finish",
    )

    def placed(values, size):
        empty = jnp.zeros_like(values)
        return jnp.where(
            is_late,
            jnp.concatenate([empty, values], axis=-1),
            jnp.concatenate([values, empty], axis=-1),
        )

    def by_heads(values):
        return placed(jnp.sum(values.reshape(heads, head_dim), axis=-1), heads)

    def by_step(values):
        return jnp.concatenate([placed(values[:heads], heads), placed(values[heads : 2 * heads], heads)])

    sum_norm, all_conv_w, all_conv_b, sum_bias, sum_alog, sum_skip, sum_gate = lax.psum(
        (
            gain_sum[0],
            jnp.concatenate([placed(sum_conv_w[:, :width], width), sum_conv_w[:, width:]], axis=1),
            jnp.concatenate([placed(sum_conv_b[0, :width], width), sum_conv_b[0, width:]]),
            by_step(small[0]),
            by_step(small[1]),
            by_heads(skip_sum[0]),
            placed(gate_sum[0], width),
        ),
        ("dp", "seq", "dir"),
    )

    def returned(value):
        own = lax.dynamic_slice_in_dim(value, core * shard, shard, axis=0)
        give = lax.dynamic_slice_in_dim(value, (1 - core) * shard, shard, axis=0)
        other = swapped(give)
        own, other = own.astype(F32), other.astype(F32)
        return jnp.where(is_late, other, own), jnp.where(is_late, own, other)

    out_a, out_b = returned(shard_out)
    gate_a, gate_b = returned(shard_gate)
    pre_a, pre_b = returned(shard_pre)
    owned_out = jnp.concatenate([out_a, out_b], axis=1)
    owned_in = jnp.concatenate(
        [
            gate_a, gate_b, pre_a[:, :width], pre_b[:, :width],
            pre_a[:, width:conv_width] + pre_b[:, width:conv_width],
        ],
        axis=1,
    )
    last = conv_width
    owned_dt = jnp.concatenate(
        [
            pre_a[:, last : last + heads], pre_b[:, last : last + heads],
            pre_a[:, last + heads : last + 2 * heads], pre_b[:, last + heads : last + 2 * heads],
        ],
        axis=1,
    )
    return (
        mixed, tokens_grad, sum_norm, owned_in, owned_dt, all_conv_w, all_conv_b, sum_bias,
        sum_alog, sum_skip, sum_gate, owned_out,
    )


def solution(mesh):
    weight = P(("dp", "seq", "dir"), None)
    values = P("dp", ("seq", "dir"), None)
    return jax.shard_map(
        shards,
        mesh=mesh,
        in_specs=(
            values, P("dp", None), P("dp"), P(), weight, weight, P(), P(), P(), P(), P(), P(),
            weight, values,
        ),
        out_specs=(
            values, values, P(), weight, weight, P(), P(), P(), P(), P(), P(), weight,
        ),
        check_vma=False,
    )
```

profile of v0, /device:TPU:0, one launch (start us, length us, event | category | flops | bytes accessed | tf_op | source)
XLA Modules:
  0.0 622.1 jit_solution(11092359773166878900)
XLA Ops:
  8.0 0.8 slice.159
  8.8 0.8 broadcast_select_fusion.6
  9.6 0.9 fusion.7
  11.3 0.9 collective-permute-done.3
  13.3 0.9 collective-permute-done.8
  14.9 0.8 broadcast_select_fusion.4
  16.1 0.9 collective-permute-done.9
  17.7 0.8 slice.154
  18.5 2.9 collective-permute-start
  21.4 1.1 collective-permute-start.1
  23.1 0.8 fusion.9
  24.1 0.8 fusion.8
  29.5 45.1 %all-gather.4.cloned.1.call-done.w_pre = bf16[768,1152]{1,0:T(8,128)(2,1)} async-done(((bf16[48,1152]{1,0:T(8,128)(2,1)}), bf16[768,1152]{1,0:T(8,128)(2,1)}) %all-gather.4.cloned.1.call-update) | async-done | bytes 1769488 | tf_op jit(solution)/shard_map/all_gather | solution.py:672
  74.6 12.1 %front.1 = (bf16[2,336,768]{2,1,0:T(8,128)(2,1)}, bf16[2,336,1024]{2,1,0:T(8,128)(2,1)}, bf16[2,320,1024]{2,1,0:T(8,128)(2,1)}, f32[2,320,1024]{2,1,0:T(8,128)},...) custom-call(s32[1,4]{1,0:T(1,128)} %add_bitcast_fusion.info, ...), custom_call_target="tpu_custom_call" | custom-call | flops 1132462080 | bytes 15093816 | tf_op jit(solution)/shard_map/front/pallas_call | solution.py:569
  86.7 1.1 select_bitcast_fusion.5
  87.8 1.2 collective-permute-start.5
  89.0 2.2 collective-permute-start.6
  92.7 7.3 %inner.1.y_in = f32[2,2,320,768]{3,2,1,0:T(8,128)} custom-call(s32[1,4]{1,0:T(1,128)} %add_bitcast_fusion.info, s32[2,4]{1,0:T(2,128)} %starts.9, bf16[2,320,1024]{2,1,0:T(8,128)(2,1)} %get-tuple-element.51.xbc, f32[2,5,320,128]{3,2,1,0:T(8,128)} %get-tuple-element.52.tab, f32[2,2,24,160]{3,2,1,0:T(8,128)} %get-tuple-element.53.cumt, ...), custom_call_target="tpu_custom_call" | custom-call | flops 629145600 | bytes 8908848 | tf_op jit(solution)/shard_map/inner/pallas_call | solution.py:569
  100.0 7.6 %collective-permute-done.5 = bf16[2,80,768]{2,1,0:T(8,128)(2,1)S(1)} collective-permute-done((bf16[2,80,768]{2,1,0:T(8,128)(2,1)S(1)}, bf16[2,80,768]{2,1,0:T(8,128)(2,1)S(1)}, u32[]{:S(2)}, u32[]{:S(2)}) %collective-permute-start.5) | collective-permute-done | bytes 245792 | tf_op jit(solution)/shard_map/ppermute | solution.py:597
  107.6 0.9 pad_maximum_fusion.received
  108.6 30.8 %all-gather.6.cloned.1.call-done.w_gate = bf16[768,768]{1,0:T(8,128)(2,1)} async-done(((bf16[48,768]{1,0:T(8,128)(2,1)}), bf16[768,768]{1,0:T(8,128)(2,1)}) %all-gather.6.cloned.1.call-update) | async-done | bytes 1179664 | tf_op jit(solution)/shard_map/all_gather | solution.py:672
  139.4 57.8 %all-gather.8.cloned.1.call-done.w_out = bf16[768,768]{1,0:T(8,128)(2,1)} async-done(((bf16[48,768]{1,0:T(8,128)(2,1)}), bf16[768,768]{1,0:T(8,128)(2,1)}) %all-gather.8.cloned.1.call-update) | async-done | bytes 1179664 | tf_op jit(solution)/shard_map/all_gather | solution.py:672
  197.2 9.0 %outer.1 = (f32[2,2,320,768]{3,2,1,0:T(8,128)}, f32[2,2,2,64,768]{4,3,2,1,0:T(8,128)}, f32[2,320,128]{2,1,0:T(8,128)}, f32[2,320,768]{2,1,0:T(8,128)}, f32[2,320...) custom-call(s32[1,4]{1,0:T(1,128)} %add_bitcast_fusion.info, s32[2,4]{1,0:T(2,128)} %starts.9, s32[2,1]{1,0:T(2,128)} %copy.28.pads, ...), custom_call_target="tpu_custom_call" | custom-call | flops 1509949440 | bytes 24516664 | tf_op jit(solution)/shard_map/outer/pallas_call | solution.py:569
  206.3 1.8 collective-permute-done.10.others
  208.9 15.3 %turn.1 = (bf16[2,320,768]{2,1,0:T(8,128)(2,1)}, bf16[2,320,768]{2,1,0:T(8,128)(2,1)}, f32[2,2,2,64,768]{4,3,2,1,0:T(8,128)}, bf16[2,2,80,768]{3,2,1,0:T(8,128)(...) custom-call(f32[2,320,128]{2,1,0:T(8,128)} %get-tuple-element.56.sum, ...), custom_call_target="tpu_custom_call" | custom-call | flops 2264924160 | bytes 23228416 | tf_op jit(solution)/shard_map/turn/pallas_call | solution.py:569
  225.8 2.3 collective-permute-start.12
  228.1 1.1 collective-permute-start.13
  229.2 15.5 %inner_back.1 = (f32[2,2,320,768]{3,2,1,0:T(8,128)}, f32[2,320,256]{2,1,0:T(8,128)}, f32[2,320,128]{2,1,0:T(8,128)}) custom-call(s32[1,4]{1,0:T(1,128)} %add_bitcast_fusion.info, s32[2,4]{1,0:T(2,128)} %starts.9, bf16[2,320,1024]{2,1,0:T(8,128)(2,1)} %get-tuple-element.51.xbc, f32[2,5,320,128]{3,2,1,0:T(8,128)} %get-tuple-element.52.tab, ...), custom_call_target="tpu_custom_call" | custom-call | flops 1258291200 | bytes 16379952 | tf_op jit(solution)/shard_map/inner_back/pallas_call | solution.py:569
  244.8 2.3 collective-permute-done.12
  247.1 1.0 pad_maximum_fusion.1.received
  248.1 24.3 %back.1 = (bf16[768,1152]{1,0:T(8,128)(2,1)}, f32[2,336,768]{2,1,0:T(8,128)}, f32[4,1024]{1,0:T(4,128)}, f32[1,1024]{1,0:T(1,128)}, f32[8,128]{1,0:T(8,128)}) custom-call(s32[1,4]{1,0:T(1,128)} %add_bitcast_fusion.info, s32[2,4]{1,0:T(2,128)} %starts.9, bf16[3,2,80,768]{3,2,1,0:T(8,128)(2,1)} %pad_maximum_fusion.1.received, ...), custom_call_target="tpu_custom_call" | custom-call | flops 3397386240 | bytes 27733552 | tf_op jit(solution)/shard_map/back/pallas_call | solution.py:569
  272.5 1.4 dynamic-slice_convert_fusion
  274.3 2.3 constant_dynamic-slice_fusion.3.branch
  276.6 5.7 collective-permute-start.15
  283.5 1.0 constant_dynamic-slice_fusion.4.dn
  284.8 1.2 collective-permute-done.16.rim_b
  286.8 0.8 copy-done.3
  287.6 3.4 finish.1
  291.8 40.8 %all-reduce.16 = (f32[768]{0:T(1024)}, f32[4,1792]{1,0:T(4,128)}, f32[1792]{0:T(1024)}, f32[48]{0:T(128)}, f32[48]{0:T(128)}, /*index=5*/f32[24]{0:T(128)}, f32[1536]{0:T(1024)}) all-reduce(f32[768]{0:T(1024)S(1)} %reduce, f32[4,1792]{1,0:T(4,128)S(1)} %pad_maximum_fusion.3, ...), channel_id=1, replica_groups=mesh['dp'=4,'seq'=4,'dir'=2] {'dp','seq','dir'}, use_global_device_ids=true, to_apply=%region_0.1 | all-reduce | flops 11384 | bytes 91072 | tf_op jit(solution)/shard_map/psum | solution.py:894
  332.6 21.6 %reduce-scatter.4.cloned.1.call-done = bf16[48,768]{1,0:T(8,128)(2,1)} async-done(((bf16[768,768]{1,0:T(8,128)(2,1)}), bf16[48,768]{1,0:T(8,128)(2,1)}) %reduce-scatter.4.cloned.1.call-update) | async-done | bytes 73744 | tf_op jit(solution)/shard_map/reduce_scatter | solution.py:797
  354.1 0.8 constant_dynamic-slice_fusion.2
  354.9 127.2 %reduce-scatter.8.cloned.1.call-done = bf16[48,768]{1,0:T(8,128)(2,1)} async-done(((bf16[768,768]{1,0:T(8,128)(2,1)}), bf16[48,768]{1,0:T(8,128)(2,1)}) %reduce-scatter.8.cloned.1.call-update) | async-done | bytes 73744 | tf_op jit(solution)/shard_map/reduce_scatter | solution.py:797
  482.8 0.8 fusion
  484.0 0.8 convert_select_fusion.3
  485.5 126.0 %reduce-scatter.6.cloned.1.call-done = bf16[48,1152]{1,0:T(8,128)(2,1)} async-done(((bf16[768,1152]{1,0:T(8,128)(2,1)}), bf16[48,1152]{1,0:T(8,128)(2,1)}) %reduce-scatter.6.cloned.1.call-update) | async-done | bytes 110608 | tf_op jit(solution)/shard_map/reduce_scatter | solution.py:797
  611.5 0.8 constant_dynamic-slice_fusion.1
  612.3 0.8 fusion.1
  613.5 0.8 convert_select_fusion
  (141 shorter events, 20.2 us)
Async XLA Ops:
  7.2 18.5 %slice-start = ((f32[4,1792]{1,0:T(4,128)}), f32[4,1536]{1,0:T(4,128)S(1)}, s32[]{:S(2)}) async-start(f32[4,1792]{1,0:T(4,128)} %param.20), calls=%async_computation.9 | async-start | bytes 49152 | tf_op jit(solution)/shard_map/slice | solution.py:685
  7.2 19.2 %slice-start.1 = ((f32[4,1792]{1,0:T(4,128)}), f32[4,256]{1,0:T(4,128)S(1)}, s32[]{:S(2)}) async-start(f32[4,1792]{1,0:T(4,128)} %param.20), calls=%async_computation.10 | async-start | bytes 8192 | tf_op jit(solution)/shard_map/slice | solution.py:685
  7.2 17.8 %copy-start.12 = (f32[1792]{0:T(1024)S(1)}, f32[1792]{0:T(1024)}, u32[]{:S(2)}) copy-start(f32[1792]{0:T(1024)} %param.21) | copy-start | bytes 21508
  7.2 20.4 %copy-start.18 = (s32[2]{0:T(128)S(1)}, s32[2]{0:T(128)}, u32[]{:S(2)}) copy-start(s32[2]{0:T(128)} %param.16) | copy-start | bytes 28
  7.2 21.1 %copy-start.11 = (f32[768]{0:T(1024)S(1)}, f32[768]{0:T(1024)}, u32[]{:S(2)}) copy-start(f32[768]{0:T(1024)} %param.17) | copy-start | bytes 9220
  7.2 67.3 %all-gather.4.cloned.1.call-start = ((), (), s32[]{:S(2)}) async-start(), calls=%async_computation.3 | async-start | bytes 1880064 | tf_op jit(solution)/shard_map/all_gather | solution.py:672
  10.8 1.4 collective-permute-start.3
  12.9 126.5 %all-gather.6.cloned.1.call-start = ((), (), s32[]{:S(2)}) async-start(), calls=%async_computation.4 | async-start | bytes 1253376 | tf_op jit(solution)/shard_map/all_gather | solution.py:672
  12.9 1.3 collective-permute-start.8
  14.9 182.3 %all-gather.8.cloned.1.call-start = ((), (), s32[]{:S(2)}) async-start(), calls=%async_computation.5 | async-start | bytes 1253376 | tf_op jit(solution)/shard_map/all_gather | solution.py:672
  15.7 1.3 collective-permute-start.9
  17.7 336.5 %reduce-scatter.4.cloned.1.call-start = ((), (), s32[]{:S(2)}) async-start(), calls=%async_computation.6 | async-start | bytes 1253376 | tf_op jit(solution)/shard_map/reduce_scatter | solution.py:797
  18.5 10.3 %collective-permute-start = (bf16[2,16,768]{2,1,0:T(8,128)(2,1)S(1)}, bf16[2,16,768]{2,1,0:T(8,128)(2,1)S(1)}, u32[]{:S(2)}, u32[]{:S(2)}) collective-permute-start(bf16[2,16,768]{2,1,0:T(8,128)(2,1)S(1)} %slice.154), channel_id=1, source_target_pairs={{0,2},{1,3},{2,4},{3,5},{4,6},{5,7},{6,0},{7,1},{8,10},{9,11},{10,... | collective-permute-start | bytes 147464 | tf_op jit(solution)/shard_map/ppermute | solution.py:606
  21.4 7.4 %collective-permute-start.1 = (bf16[2,16,768]{2,1,0:T(8,128)(2,1)S(1)}, bf16[2,16,768]{2,1,0:T(8,128)(2,1)S(1)}, u32[]{:S(2)}, u32[]{:S(2)}) collective-permute-start(bf16[2,16,768]{2,1,0:T(8,128)(2,1)S(1)} %slice.154), channel_id=1, source_target_pairs={{0,3},{1,2},{2,5},{3,4},{4,7},{5,6},{6,1},{7,0},{8,11},{9,10},{10,... | collective-permute-start | bytes 147464 | tf_op jit(solution)/shard_map/ppermute | solution.py:606
  22.5 7.0 %collective-permute-start.2 = (bf16[2,160,768]{2,1,0:T(8,128)(2,1)}, bf16[2,160,768]{2,1,0:T(8,128)(2,1)S(1)}, u32[]{:S(2)}, u32[]{:S(2)}) collective-permute-start(bf16[2,160,768]{2,1,0:T(8,128)(2,1)} %own.3), channel_id=1, source_target_pairs={{0,1},{1,0},{2,3},{3,2},{4,5},{5,4},{6,7},{7,6},{8,9},{9,8},{10,11... | collective-permute-start | bytes 1474568 | tf_op jit(solution)/shard_map/ppermute | solution.py:592
  23.1 85.4 %collective-permute-start.7 = (bf16[2,160,768]{2,1,0:T(8,128)(2,1)}, bf16[2,160,768]{2,1,0:T(8,128)(2,1)S(1)}, u32[]{:S(2)}, u32[]{:S(2)}) collective-permute-start(bf16[2,160,768]{2,1,0:T(8,128)(2,1)} %cot.1), channel_id=1, source_target_pairs={{0,1},{1,0},{2,3},{3,2},{4,5},{5,4},{6,7},{7,6},{8,9},{9,8},{10,11... | collective-permute-start | bytes 1474568 | tf_op jit(solution)/shard_map/ppermute | solution.py:592
  29.5 45.1 %copy-start.17 = (bf16[2,160,768]{2,1,0:T(8,128)(2,1)}, bf16[2,160,768]{2,1,0:T(8,128)(2,1)S(1)}, u32[]{:S(2)}) copy-start(bf16[2,160,768]{2,1,0:T(8,128)(2,1)S(1)} %collective-permute-done.2.other) | copy-start | bytes 1474564
  74.6 16.6 %copy-start.19 = (f32[24]{0:T(128)S(1)}, f32[24]{0:T(128)}, u32[]{:S(2)}) copy-start(f32[24]{0:T(128)} %param.24) | copy-start | bytes 292
  74.6 17.4 %copy-start.15 = (f32[1536]{0:T(1024)S(1)}, f32[1536]{0:T(1024)}, u32[]{:S(2)}) copy-start(f32[1536]{0:T(1024)} %param.25) | copy-start | bytes 18436
  87.8 19.8 %collective-permute-start.5 = (bf16[2,80,768]{2,1,0:T(8,128)(2,1)S(1)}, bf16[2,80,768]{2,1,0:T(8,128)(2,1)S(1)}, u32[]{:S(2)}, u32[]{:S(2)}) collective-permute-start(bf16[2,80,768]{2,1,0:T(8,128)(2,1)S(1)} %get-tuple-element.96), channel_id=1, source_target_pairs={{0,4},{2,6},{4,0},{6,2},{1,5},{3,7},{5,1},{7,3},{8,12},{10,14},{12... | collective-permute-start | bytes 737288 | tf_op jit(solution)/shard_map/ppermute | solution.py:597
  89.0 18.6 %collective-permute-start.6 = (bf16[2,80,768]{2,1,0:T(8,128)(2,1)S(1)}, bf16[2,80,768]{2,1,0:T(8,128)(2,1)S(1)}, u32[]{:S(2)}, u32[]{:S(2)}) collective-permute-start(bf16[2,80,768]{2,1,0:T(8,128)(2,1)S(1)} %get-tuple-element.95), channel_id=1, source_target_pairs={{0,6},{2,0},{4,2},{6,4},{1,7},{3,1},{5,3},{7,5},{8,14},{10,8},{12,... | collective-permute-start | bytes 737288 | tf_op jit(solution)/shard_map/ppermute | solution.py:597
  91.2 16.4 %collective-permute-start.4 = (bf16[2,80,768]{2,1,0:T(8,128)(2,1)S(1)}, bf16[2,80,768]{2,1,0:T(8,128)(2,1)S(1)}, u32[]{:S(2)}, u32[]{:S(2)}) collective-permute-start(bf16[2,80,768]{2,1,0:T(8,128)(2,1)S(1)} %get-tuple-element.94), channel_id=1, source_target_pairs={{0,2},{2,4},{4,6},{6,0},{1,3},{3,5},{5,7},{7,1},{8,10},{10,12},{12... | collective-permute-start | bytes 737288 | tf_op jit(solution)/shard_map/ppermute | solution.py:597
  108.6 88.7 %copy-start.1 = (bf16[2,160,768]{2,1,0:T(8,128)(2,1)}, bf16[2,160,768]{2,1,0:T(8,128)(2,1)S(1)}, u32[]{:S(2)}) copy-start(bf16[2,160,768]{2,1,0:T(8,128)(2,1)S(1)} %collective-permute-done.7.cot_other) | copy-start | bytes 1474564
  206.2 1.9 collective-permute-start.10
  208.1 0.8 copy-start.5
  224.2 1.0 copy-start.4
  224.3 257.8 %reduce-scatter.8.cloned.1.call-start = ((), (), s32[]{:S(2)}) async-start(), calls=%async_computation.8 | async-start | bytes 1253376 | tf_op jit(solution)/shard_map/reduce_scatter | solution.py:797
  224.9 386.6 %reduce-scatter.6.cloned.1.call-start = ((), (), s32[]{:S(2)}) async-start(), calls=%async_computation.7 | async-start | bytes 1880064 | tf_op jit(solution)/shard_map/reduce_scatter | solution.py:797
  225.3 19.4 %collective-permute-start.11 = (bf16[2,80,768]{2,1,0:T(8,128)(2,1)S(1)}, bf16[2,80,768]{2,1,0:T(8,128)(2,1)S(1)}, u32[]{:S(2)}, u32[]{:S(2)}) collective-permute-start(bf16[2,80,768]{2,1,0:T(8,128)(2,1)S(1)} %get-tuple-element.91), channel_id=1, source_target_pairs={{0,2},{2,4},{4,6},{6,0},{1,3},{3,5},{5,7},{7,1},{8,10},{10,12},{12... | collective-permute-start | bytes 737288 | tf_op jit(solution)/shard_map/ppermute | solution.py:597
  225.8 21.3 %collective-permute-start.12 = (bf16[2,80,768]{2,1,0:T(8,128)(2,1)S(1)}, bf16[2,80,768]{2,1,0:T(8,128)(2,1)S(1)}, u32[]{:S(2)}, u32[]{:S(2)}) collective-permute-start(bf16[2,80,768]{2,1,0:T(8,128)(2,1)S(1)} %get-tuple-element.93), channel_id=1, source_target_pairs={{0,4},{2,6},{4,0},{6,2},{1,5},{3,7},{5,1},{7,3},{8,12},{10,14},{12... | collective-permute-start | bytes 737288 | tf_op jit(solution)/shard_map/ppermute | solution.py:597
  228.1 19.0 %collective-permute-start.13 = (bf16[2,80,768]{2,1,0:T(8,128)(2,1)S(1)}, bf16[2,80,768]{2,1,0:T(8,128)(2,1)S(1)}, u32[]{:S(2)}, u32[]{:S(2)}) collective-permute-start(bf16[2,80,768]{2,1,0:T(8,128)(2,1)S(1)} %get-tuple-element.92), channel_id=1, source_target_pairs={{0,6},{2,0},{4,2},{6,4},{1,7},{3,1},{5,3},{7,5},{8,14},{10,8},{12,... | collective-permute-start | bytes 737288 | tf_op jit(solution)/shard_map/ppermute | solution.py:597
  272.4 1.6 copy-start.14
  272.4 1.8 copy-start.13
  272.4 4.1 copy-start.9
  272.4 4.1 copy-start
  272.4 10.3 %copy-start.10 = (f32[1,1024]{1,0:T(1,128)S(1)}, f32[1,1024]{1,0:T(1,128)}, u32[]{:S(2)}) copy-start(f32[1,1024]{1,0:T(1,128)} %get-tuple-element.79) | copy-start | bytes 12292
  272.4 10.7 %copy-start.16 = (f32[8,128]{1,0:T(8,128)S(1)}, f32[8,128]{1,0:T(8,128)}, u32[]{:S(2)}) copy-start(f32[8,128]{1,0:T(8,128)} %get-tuple-element.80) | copy-start | bytes 12292
  273.9 12.2 %collective-permute-start.17 = (bf16[2,160,768]{2,1,0:T(8,128)(2,1)S(1)}, bf16[2,160,768]{2,1,0:T(8,128)(2,1)S(1)}, u32[]{:S(2)}, u32[]{:S(2)}) collective-permute-start(bf16[2,160,768]{2,1,0:T(8,128)(2,1)S(1)} %dynamic-slice_convert_fusion), channel_id=1, source_target_pairs={{0,1},{1,0},{2,3},{3,2},{4,5},{5,4},{6,7},{7,6},{8,9},{9,8},{10,11... | collective-permute-start | bytes 1474568 | tf_op jit(solution)/shard_map/ppermute | solution.py:592
  276.6 8.3 %collective-permute-start.15 = (bf16[2,16,768]{2,1,0:T(8,128)(2,1)S(1)}, bf16[2,16,768]{2,1,0:T(8,128)(2,1)S(1)}, u32[]{:S(2)}, u32[]{:S(2)}) collective-permute-start(bf16[2,16,768]{2,1,0:T(8,128)(2,1)S(1)} %slice.240), channel_id=1, source_target_pairs={{0,6},{1,7},{2,0},{3,1},{4,2},{5,3},{6,4},{7,5},{8,14},{9,15},{10,... | collective-permute-start | bytes 147464 | tf_op jit(solution)/shard_map/ppermute | solution.py:606
  282.3 3.7 collective-permute-start.16
  282.7 3.3 collective-permute-start.14
  284.8 1.2 copy-start.6
  286.0 0.8 copy-start.2
  286.8 0.8 copy-start.3
  354.9 127.9 %collective-permute-start.18 = (bf16[24,768]{1,0:T(8,128)(2,1)S(1)}, bf16[24,768]{1,0:T(8,128)(2,1)S(1)}, u32[]{:S(2)}, u32[]{:S(2)}) collective-permute-start(bf16[24,768]{1,0:T(8,128)(2,1)S(1)} %constant_dynamic-slice_fusion.2), channel_id=1, source_target_pairs={{0,1},{1,0},{2,3},{3,2},{4,5},{5,4},{6,7},{7,6},{8,9},{9,8},{10,11... | collective-permute-start | bytes 110600 | tf_op jit(solution)/shard_map/ppermute | solution.py:592
  482.8 1.2 collective-permute-start.20
  612.3 1.2 collective-permute-start.19
  614.5 0.7 copy-start.8
  (1 other events, 0.6 us)
Sparse Core Ops, SparseCore 0:
  13.0 61.5 all-gather.3
  77.3 61.9 all-gather.5
  142.1 55.0 all-gather.7
  224.4 129.6 reduce-scatter.3
  358.7 123.2 reduce-scatter.7
  486.8 124.6 reduce-scatter.5
where the time goes:
time: 623 us; the launch traced here: 622 us
  waiting for transfers between devices  426 us (68%)
  Pallas kernels  87 us (14%)
  blocking collectives  40.8 us (7%)
  starting transfers between devices  20.1 us (3%)
  local copies, waits for them, and re-layouts  18.3 us (3%)
  other arithmetic  15.6 us (3%)
  between operations  14.5 us (2%)
    reduce_scatter x3, waiting for transfers between devices, reduced(): lax.psum_scatter(grad, ('dp', 'seq'), scatter_dimension=0, tiled=True)  275 us
    all_gather x3, waiting for transfers between devices, gathered(): lax.all_gather(both(keep, swapped(give)), ('dp', 'seq'), axis=0, tiled=True)  134 us
    pallas_call x7, Pallas kernels, run(): pl.pallas_call(body, grid=grid, out_shape=[s for s, _ in outs], in_specs=...  87 us
    psum x1, blocking collectives, shards(): lax.psum((gain_sum[0], jnp.concatenate([placed(sum_conv_w[:, :width], wid...  40.8 us
  transfers between devices with their start and end apart: 27, of which 16 were waited for; matrix products, arithmetic and copies ran while one was open for 4% of the time, Pallas kernels for 10%

commit v1 on v0

--- a/solution.py
+++ b/solution.py
@@ -310,7 +310,7 @@
     dy_o[0] = dy
     dz_o[0] = dz
     dy_f = dy.astype(F32)
-    branch_o[0] = dot_nt(gated, w_out[...])
+    branch_o[0] = dot_nt(gated, w_out[...]).astype(BF)
 
     @pl.when(row == 0)
     def _():
@@ -509,8 +509,8 @@
     d_all = jnp.concatenate([d_pre.astype(BF), d_raws], axis=1)
     acc[...] += dot_tn(normed[0], d_all)
     dn = dot_nt(d_all, w_pre[...])
-    dn_o[0, 0:HALO] = dn[0:HALO]
-    dn_o[0, HALO:] = dn[HALO:] + dot_nt(dz[0], w_gate[...])
+    dn_o[0, 0:HALO] = dn[0:HALO].astype(BF)
+    dn_o[0, HALO:] = (dn[HALO:] + dot_nt(dz[0], w_gate[...])).astype(BF)
 
     @pl.when(row == pl.num_programs(0) - 1)
     def _():
@@ -526,8 +526,8 @@
     x = own[0].astype(F32)
     places = column_places(half, base + core * half)
     valid = (places < row_len - pads[row, 0]).astype(F32)
-    mixed_o[0] = (x + valid * (branch[0] + branch_other[0].astype(F32))).astype(BF)
-    ds[...] = dn[0] + dn_other[0].astype(F32)
+    mixed_o[0] = (x + valid * (branch[0].astype(F32) + branch_other[0].astype(F32))).astype(BF)
+    ds[...] = dn[0].astype(F32) + dn_other[0].astype(F32)
     takes = ((core == 1) & (place + 1 < count)).astype(F32)
     ds[half - HALO :] += takes * (rim_a[0].astype(F32) + rim_b[0].astype(F32))
     d_normed = ds[...]
@@ -544,7 +544,448 @@
     gain_o[...] += jnp.sum(d_normed * x * scale, axis=0, keepdims=True)
 
 
+MESH = pl.DeviceIdType.MESH
+
+
+def remote(src, dst, send_sem, recv_sem, device):
+    return pltpu.make_async_remote_copy(
+        src_ref=src, dst_ref=dst, send_sem=send_sem, recv_sem=recv_sem, device_id=device,
+        device_id_type=MESH,
+    )
+
+
+class Sender:
+    def __init__(self, send_sems, recv_sems):
+        self.send_sems, self.recv_sems = send_sems, recv_sems
+        self.sent = 0
+        self.slots = 0
+        self.pending = []
+
+    def slot(self):
+        self.slots += 1
+        return self.slots - 1
+
+    def send(self, src, dst, slot, device):
+        copy = remote(src, dst, self.send_sems.at[self.sent], self.recv_sems.at[slot], device)
+        self.sent += 1
+        copy.start()
+        self.pending.append(copy)
+
+    def arrive(self, dst, slot, device):
+        remote(dst, dst, self.send_sems.at[0], self.recv_sems.at[slot], device).wait_recv()
+
+    def drain(self):
+        for copy in self.pending:
+            copy.wait_send()
+        self.pending = []
+
+
+class Place:
+    def __init__(self, count):
+        self.dp, self.seq, self.dir = (lax.axis_index(a) for a in ("dp", "seq", "dir"))
+        self.count = count
+        self.side = self.dp + 1 - 2 * (self.dp % 2)
+        self.below = (self.dp + 2) % 4
+        self.across = 3 - self.dp
+        self.me = (self.dp, self.seq, self.dir)
+        self.sibling = (self.dp, self.seq, 1 - self.dir)
+        self.by_x = (self.side, self.seq, self.dir)
+        self.by_y = (self.below, self.seq, self.dir)
+
+    def along(self, k, crossed=False):
+        core = 1 - self.dir if crossed else self.dir
+        return (self.dp, (self.seq + k + self.count) % self.count, core)
+
+    def at(self, k):
+        return (self.seq + k + self.count) % self.count
+
+    def chip(self, dp, k=0):
+        return dp * self.count + self.at(k)
+
+    def meet(self):
+        barrier = pltpu.get_barrier_semaphore()
+        others = [self.sibling, self.by_x, self.by_y]
+        others += [self.along(k) for k in range(1, self.count)]
+        others += [self.along(1, True), self.along(-1, True)]
+        for device in others:
+            pl.semaphore_signal(barrier, inc=1, device_id=device, device_id_type=MESH)
+        pl.semaphore_wait(barrier, len(others))
+
+
+class Spread:
+    def __init__(self, place, sender, slab, cut):
+        self.place, self.sender, self.slab, self.cut = place, sender, slab, cut
+        count = place.count
+        self.z = [None] + [sender.slot() for _ in range(1, count)]
+        self.x, self.y, self.xd, self.yd = (
+            [sender.slot() for _ in range(count)] for _ in range(4)
+        )
+
+    def start(self, mine):
+        here, to = self.place, self.sender
+        spot = self.slab.at[here.chip(here.dp)]
+        to.send(mine, spot, self.x[0], here.by_x)
+        to.send(mine, spot, self.y[0], here.by_y)
+        for k in range(1, here.count):
+            to.send(mine, spot, self.z[k], here.along(k))
+
+    def relay(self, k):
+        here, to = self.place, self.sender
+        spot = self.slab.at[here.chip(here.dp, -k)]
+        to.arrive(spot, self.z[k], here.along(-k))
+        to.send(spot, spot, self.x[k], here.by_x)
+        to.send(spot, spot, self.y[k], here.by_y)
+
+    def cross(self, k):
+        here, to = self.place, self.sender
+        from_x = self.slab.at[here.chip(here.side, -k)]
+        to.arrive(from_x, self.x[k], here.by_x)
+        part = from_x.at[:, : self.cut]
+        to.send(part, part, self.yd[k], here.by_y)
+        from_y = self.slab.at[here.chip(here.below, -k)]
+        to.arrive(from_y, self.y[k], here.by_y)
+        part = from_y.at[:, self.cut :]
+        to.send(part, part, self.xd[k], here.by_x)
+
+    def end(self, k):
+        here, to = self.place, self.sender
+        spot = self.slab.at[here.chip(here.across, -k)]
+        to.arrive(spot.at[:, : self.cut], self.yd[k], here.by_y)
+        to.arrive(spot.at[:, self.cut :], self.xd[k], here.by_x)
+
+
+def gather_copies(count):
+    return 6 + 2 * ((count - 1) + 4 * count)
+
+
+def gather(dims, count, cuts, w_in, w_dt, w_out, tokens, cot, pre_o, late_o, tokens_o, cot_o, halo_o,
+           give_pre, give_late, got_pre, got_late, pre_mine, late_mine, send_sems, recv_sems, own_sems):
+    heads, head_dim, state, _ = dims
+    width = heads * head_dim
+    half = tokens.shape[1]
+    here = Place(count)
+    to = Sender(send_sems, recv_sems)
+    shard = w_in.shape[0]
+    late_core = here.dir == 1
+    conv_width = width + 4 * state
+    source = lax.broadcasted_iota(jnp.int32, (4 * heads, LANES), 0)
+    lane = lax.broadcasted_iota(jnp.int32, (4 * heads, LANES), 1)
+
+    def fill(core, pre, late):
+        late_side = core == 1
+        pick = lambda ref, at: jnp.where(
+            late_side, ref[:, at + width : at + 2 * width], ref[:, at : at + width]
+        )
+        pre[:, 0:width] = pick(w_in, 2 * width).astype(pre.dtype)
+        pre[:, width:conv_width] = w_in[:, 4 * width :].astype(pre.dtype)
+        column = jnp.where(lane < heads, lane, lane + heads) + core * heads
+        ones = jnp.where((source == column) & (lane < 2 * heads), 1.0, 0.0).astype(BF)
+        pre[:, conv_width:] = dot(w_dt[...], ones).astype(pre.dtype)
+        late[:, 0:width] = pick(w_in, 0).astype(late.dtype)
+        late[:, width:] = pick(w_out, 0).astype(late.dtype)
+
+    fill(1 - here.dir, give_pre, give_late)
+    here.meet()
+    slots = [to.slot() for _ in range(5)]
+    to.send(give_pre, got_pre, slots[0], here.sibling)
+    to.send(give_late, got_late, slots[1], here.sibling)
+    to.send(tokens, tokens_o, slots[2], here.sibling)
+    to.send(cot, cot_o, slots[3], here.sibling)
+    rim = tokens.at[:, pl.ds(half - HALO, HALO)]
+    first_rim, second_rim = to.sent, to.sent + 1
+    to.sent += 2
+
+    @pl.when(late_core)
+    def _():
+        for sem, crossed in ((first_rim, False), (second_rim, True)):
+            remote(
+                rim, halo_o, send_sems.at[sem], recv_sems.at[slots[4]], here.along(1, crossed)
+            ).start()
+
+    pre_spread = Spread(here, to, pre_o, cuts[0])
+    late_spread = Spread(here, to, late_o, cuts[1])
+    fill(here.dir, pre_mine, late_mine)
+
+    def joined(own, got):
+        other = got[...].astype(F32)
+        own = own[...]
+        return jnp.where(
+            late_core,
+            jnp.concatenate([other, own], axis=0),
+            jnp.concatenate([own, other], axis=0),
+        ).astype(BF)
+
+    return here, to, slots, rim, first_rim, second_rim, pre_spread, late_spread, joined
+
+
+def gather_all(dims, count, cuts, w_in, w_dt, w_out, tokens, cot, pre_o, late_o, tokens_o, cot_o,
+               halo_o, give_pre, give_late, got_pre, got_late, pre_mine, late_mine, pre_block,
+               late_block, send_sems, recv_sems, own_sems):
+    here, to, slots, rim, first_rim, second_rim, pre_spread, late_spread, joined = gather(
+        dims, count, cuts, w_in, w_dt, w_out, tokens, cot, pre_o, late_o, tokens_o, cot_o, halo_o,
+        give_pre, give_late, got_pre, got_late, pre_mine, late_mine, send_sems, recv_sems, own_sems)
+    to.arrive(got_pre, slots[0], here.sibling)
+    pre_block[...] = joined(pre_mine, got_pre)
+    pre_spread.start(pre_block)
+    to.arrive(got_late, slots[1], here.sibling)
+    late_block[...] = joined(late_mine, got_late)
+    keep = [
+        pltpu.make_async_copy(block, slab.at[here.chip(here.dp)], own_sems.at[i])
+        for i, (block, slab) in enumerate(((pre_block, pre_o), (late_block, late_o)))
+    ]
+    for copy in keep:
+        copy.start()
+    late_spread.start(late_block)
+    for spread in (pre_spread, late_spread):
+        spread.cross(0)
+        for k in range(1, count):
+            spread.relay(k)
+            spread.cross(k)
+    for spread in (pre_spread, late_spread):
+        for k in range(count):
+            spread.end(k)
+    to.arrive(tokens_o, slots[2], here.sibling)
+    to.arrive(cot_o, slots[3], here.sibling)
+    to.arrive(halo_o, slots[4], here.along(-1))
+    for copy in keep:
+        copy.wait()
+    to.drain()
+
+    @pl.when(here.dir == 1)
+    def _():
+        for sem, crossed in ((first_rim, False), (second_rim, True)):
+            remote(
+                rim, halo_o, send_sems.at[sem], recv_sems.at[slots[4]], here.along(1, crossed)
+            ).wait_send()
+
+
+class Reduce:
+    def __init__(self, place, sender, grad, cut, first, second, third, out_second, out_third, total):
+        self.place, self.sender, self.grad, self.cut = place, sender, grad, cut
+        self.first, self.second, self.third = first, second, third
+        self.out_second, self.out_third, self.total = out_second, out_third, total
+        count = place.count
+        self.one = [[[sender.slot() for _ in range(count)] for _ in range(2)] for _ in range(2)]
+        self.two = [[sender.slot() for _ in range(count)] for _ in range(2)]
+        self.three = [None] + [sender.slot() for _ in range(1, count)]
+        self.sides = (slice(0, cut), slice(cut, grad.shape[2]))
+
+    def start(self, k):
+        here, to = self.place, self.sender
+        for side, device, targets in (
+            (0, here.by_x, (here.side, here.across)),
+            (1, here.by_y, (here.below, here.across)),
+        ):
+            at = self.sides[side]
+            for q in (1, 0):
+                to.send(
+                    self.grad.at[here.chip(targets[q], k), :, at],
+                    self.first.at[q, k, :, at],
+                    self.one[side][q][k], device,
+                )
+
+    def pass_on(self, k):
+        here, to = self.place, self.sender
+        for side, came, device, target in (
+            (0, here.by_x, here.by_y, here.below),
+            (1, here.by_y, here.by_x, here.side),
+        ):
+            at = self.sides[side]
+            to.arrive(self.first.at[1, k, :, at], self.one[side][1][k], came)
+            self.out_second[k, :, at] = (
+                self.grad[here.chip(target, k), :, at].astype(F32)
+                + self.first[1, k, :, at].astype(F32)
+            ).astype(BF)
+            to.send(self.out_second.at[k, :, at], self.second.at[k, :, at], self.two[side][k], device)
+
+    def along(self, k):
+        here, to = self.place, self.sender
+        for side, came, then in ((0, here.by_x, here.by_y), (1, here.by_y, here.by_x)):
+            at = self.sides[side]
+            to.arrive(self.first.at[0, k, :, at], self.one[side][0][k], came)
+            to.arrive(self.second.at[k, :, at], self.two[side][k], then)
+            summed = (
+                self.grad[here.chip(here.dp, k), :, at].astype(F32)
+                + self.first[0, k, :, at].astype(F32)
+                + self.second[k, :, at].astype(F32)
+            )
+            if k == 0:
+                self.total[:, at] = summed
+            else:
+                self.out_third[k - 1, :, at] = summed.astype(BF)
+        if k:
+            to.send(self.out_third.at[k - 1], self.third.at[k - 1], self.three[k], here.along(k))
+
+    def end(self):
+        here, to = self.place, self.sender
+        for k in range(1, here.count):
+            to.arrive(self.third.at[k - 1], self.three[k], here.along(-k))
+            self.total[...] += self.third[k - 1].astype(F32)
+
+
+def settle_copies(count):
+    per_grad = 4 * count + 2 * count + (count - 1)
+    return 3 * (per_grad + 1) + 3 + (2 + (count - 1) + 1)
+
+
+def settle(dims, count, cuts, pads, tokens, cot, gain, dn, branch, g_pre, g_gate, g_out, conv_w, conv_b,
+           gate_sum, skip_sum, small, mixed_o, grad_o, in_o, dt_o, out_o, conv_w_o, conv_b_o, gate_o,
+           skip_o, small_o, norm_o, *rest):
+    heads, head_dim, state, row_len = dims
+    width = heads * head_dim
+    conv_width = width + 4 * state
+    works = [rest[6 * i : 6 * i + 6] for i in range(3)]
+    (other_pre, other_gate, other_out, dn_other, branch_other, rims, ds, v_own, v_x, v_y, v_z, v_other,
+     send_sems, recv_sems) = rest[18:]
+    here = Place(count)
+    to = Sender(send_sems, recv_sems)
+    rows, half, model = tokens.shape
+    here.meet()
+    reduces = [
+        Reduce(here, to, grad, cut, *work)
+        for grad, cut, work in zip((g_pre, g_gate, g_out), cuts, works)
+    ]
+    for reduce in reduces:
+        for k in list(range(1, count)) + [0]:
+            reduce.start(k)
+    dn_slot, branch_slot, rim_own, rim_cross = (to.slot() for _ in range(4))
+    give = pl.multiple_of((1 - here.dir) * half, HALO)
+    keep = pl.multiple_of(here.dir * half, HALO)
+    to.send(dn.at[:, pl.ds(HALO + give, half)], dn_other, dn_slot, here.sibling)
+    to.send(branch.at[:, pl.ds(give, half)], branch_other, branch_slot, here.sibling)
+    edge = dn.at[:, pl.ds(0, HALO)]
+    rim_sem = to.sent
+    to.sent += 1
+
+    @pl.when(here.dir == 1)
+    def _():
+        remote(edge, rims.at[1], send_sems.at[rim_sem], recv_sems.at[rim_own], here.along(-1)).start()
+
+    @pl.when(here.dir == 0)
+    def _():
+        remote(
+            edge, rims.at[0], send_sems.at[rim_sem], recv_sems.at[rim_cross], here.along(-1, True)
+        ).start()
+
+    order = list(range(1, count)) + [0]
+    for reduce in reduces:
+        for k in order:
+            reduce.pass_on(k)
+    to.arrive(dn_other, dn_slot, here.sibling)
+    to.arrive(branch_other, branch_slot, here.sibling)
+
+    @pl.when(here.dir == 1)
+    def _():
+        to.arrive(rims.at[1], rim_own, here.along(1))
+        to.arrive(rims.at[0], rim_cross, here.along(1, True))
+
+    @pl.when(here.dir == 0)
+    def _():
+        rims[...] = jnp.zeros_like(rims)
+
+    gain_sum = None
+    takes = ((here.dir == 1) & (here.seq + 1 < count)).astype(F32)
+    for row in range(rows):
+        x = tokens[row].astype(F32)
+        places = column_places(half, (here.seq * 2 + here.dir) * half)
+        valid = (places < row_len - pads[row, 0]).astype(F32)
+        mixed_o[row] = (
+            x + valid * (branch[row, pl.ds(keep, half)].astype(F32) + branch_other[row].astype(F32))
+        ).astype(BF)
+        ds[...] = dn[row, pl.ds(HALO + keep, half)].astype(F32) + dn_other[row].astype(F32)
+        ds[half - HALO :] += takes * (rims[0, row].astype(F32) + rims[1, row].astype(F32))
+        d_normed = ds[...]
+        scale = lax.rsqrt(jnp.mean(x * x, axis=-1, keepdims=True) + EPSILON)
+        weighed = d_normed * gain[...]
+        along = jnp.mean(weighed * x, axis=-1, keepdims=True)
+        dx = scale * weighed - x * (scale * scale * scale * along)
+        grad_o[row] = (cot[row].astype(F32) + dx).astype(BF)
+        term = jnp.sum(d_normed * x * scale, axis=0, keepdims=True)
+        gain_sum = term if gain_sum is None else gain_sum + term
+    side = v_own.shape[1] - width
+    v_own[0:4] = conv_w[...]
+    v_own[4:5] = conv_b[...]
+    v_own[5:6] = jnp.concatenate([gate_sum[...], small[0:1], small[1:2]], axis=1)
+    v_own[6:7] = jnp.concatenate([skip_sum[...], jnp.zeros((1, side), F32)], axis=1)
+    v_own[7:8] = jnp.concatenate([gain_sum, jnp.zeros((1, side), F32)], axis=1)
+    v_slots = [to.slot() for _ in range(2 + count)]
+    to.send(v_own, v_x.at[0], v_slots[0], here.by_x)
+    for reduce in reduces:
+        for k in order:
+            reduce.along(k)
+    to.arrive(v_x.at[0], v_slots[0], here.by_x)
+    v_x[1] = v_own[...] + v_x[0]
+    to.send(v_x.at[1], v_y.at[0], v_slots[1], here.by_y)
+    to.arrive(v_y.at[0], v_slots[1], here.by_y)
+    v_y[1] = v_x[1] + v_y[0]
+    for k in range(1, count):
+        to.send(v_y.at[1], v_z.at[k - 1], v_slots[1 + k], here.along(k))
+    swaps = []
+    shard = in_o.shape[0]
+    for reduce, other in zip(reduces, (other_pre, other_gate, other_out)):
+        reduce.end()
+        slot = to.slot()
+        back_rows = pl.ds(pl.multiple_of((1 - here.dir) * shard, 8), shard)
+        to.send(reduce.total.at[back_rows], other, slot, here.sibling)
+        swaps.append((other, slot))
+    total = v_y[1]
+    for k in range(1, count):
+        to.arrive(v_z.at[k - 1], v_slots[1 + k], here.along(-k))
+        total = total + v_z[k - 1]
+    v_x[0] = total
+    to.send(v_x.at[0], v_other, v_slots[1 + count], here.sibling)
+    late = here.dir == 1
+    own_rows = pl.ds(pl.multiple_of(here.dir * shard, 8), shard)
+    sorted_parts = []
+    for reduce, (other, slot) in zip(reduces, swaps):
+        to.arrive(other, slot, here.sibling)
+        own, got = reduce.total[own_rows], other[...]
+        sorted_parts.append((jnp.where(late, got, own), jnp.where(late, own, got)))
+    (pre_a, pre_b), (gate_a, gate_b), (out_a, out_b) = sorted_parts
+    in_o[:, 0:width] = gate_a
+    in_o[:, width : 2 * width] = gate_b
+    in_o[:, 2 * width : 3 * width] = pre_a[:, :width]
+    in_o[:, 3 * width : 4 * width] = pre_b[:, :width]
+    in_o[:, 4 * width :] = pre_a[:, width:conv_width] + pre_b[:, width:conv_width]
+    dt_o[0] = pre_a[:, conv_width:]
+    dt_o[1] = pre_b[:, conv_width:]
+    out_o[:, 0:width] = out_a
+    out_o[:, width:] = out_b
+    to.arrive(v_other, v_slots[1 + count], here.sibling)
+    got = v_other[...]
+    v_a, v_b = jnp.where(late, got, total), jnp.where(late, total, got)
+    both = v_a + v_b
+    conv_w_o[:, 0:width] = v_a[0:4, :width]
+    conv_w_o[:, width : 2 * width] = v_b[0:4, :width]
+    conv_w_o[:, 2 * width :] = both[0:4, width:]
+    conv_b_o[:, 0:width] = v_a[4:5, :width]
+    conv_b_o[:, width : 2 * width] = v_b[4:5, :width]
+    conv_b_o[:, 2 * width :] = both[4:5, width:]
+    gate_o[:, 0:width] = v_a[5:6, :width]
+    gate_o[:, width:] = v_b[5:6, :width]
+    small_o[0:1] = v_a[5:6, width : width + LANES]
+    small_o[1:2] = v_a[5:6, width + LANES : width + 2 * LANES]
+    small_o[2:3] = v_b[5:6, width : width + LANES]
+    small_o[3:4] = v_b[5:6, width + LANES : width + 2 * LANES]
+    skip_o[:, 0:width] = v_a[6:7, :width]
+    skip_o[:, width:] = v_b[6:7, :width]
+    norm_o[...] = both[7:8, :model]
+    to.drain()
+
+    @pl.when(here.dir == 1)
+    def _():
+        remote(edge, rims.at[1], send_sems.at[rim_sem], recv_sems.at[rim_own], here.along(-1)).wait_send()
+
+    @pl.when(here.dir == 0)
+    def _():
+        remote(
+            edge, rims.at[0], send_sems.at[rim_sem], recv_sems.at[rim_cross], here.along(-1, True)
+        ).wait_send()
+
+
 SMEM = pl.BlockSpec(memory_space=pltpu.SMEM)
+VMEM = pl.BlockSpec(memory_space=pltpu.VMEM)
+ANY = pl.BlockSpec(memory_space=pl.ANY)
 
 
 def whole(*shape):
@@ -561,7 +1002,7 @@
     )
 
 
-def run(body, grid, ins, outs, scratch=(), flops=0, name=None):
+def run(body, grid, ins, outs, scratch=(), flops=0, name=None, collective_id=None):
     arrays = [a for a, _ in ins]
     moved = sum(a.size * a.dtype.itemsize for a in arrays) + sum(
         s.size * s.dtype.itemsize for s, _ in outs
@@ -576,6 +1017,8 @@
         compiler_params=pltpu.CompilerParams(
             vmem_limit_bytes=VMEM_BYTES,
             dimension_semantics=("arbitrary",) * len(grid),
+            collective_id=collective_id,
+            has_side_effects=collective_id is not None,
         ),
         cost_estimate=pl.CostEstimate(
             flops=flops, bytes_accessed=moved, transcendentals=flops // 500
@@ -613,6 +1056,129 @@
         chosen = jnp.where(place + k < count, value[0], value[1])
         out.append(rotated(chosen, k))
     return jnp.stack(out)
+
+
+def gathered_apart(w_in, w_dt, w_out, tokens, cotangent, heads, width, inner_width, is_late):
+    all_heads = 2 * heads
+    half = tokens.shape[1]
+    pad_dt = jnp.zeros((w_in.shape[0], LANES - 2 * heads), BF)
+
+    def columns(c):
+        return (
+            jnp.concatenate(
+                [
+                    w_in[:, inner_width + c * width : inner_width + (c + 1) * width],
+                    w_in[:, 2 * inner_width :],
+                    w_dt[:, c * heads : (c + 1) * heads],
+                    w_dt[:, all_heads + c * heads : all_heads + (c + 1) * heads],
+                    pad_dt,
+                ],
+                axis=1,
+            ),
+            jnp.concatenate(
+                [w_in[:, c * width : (c + 1) * width], w_out[:, c * width : (c + 1) * width]], axis=1
+            ),
+        )
+
+    first, latter = columns(0), columns(1)
+
+    def gathered(i):
+        keep = jnp.where(is_late, latter[i], first[i])
+        give = swapped(jnp.where(is_late, first[i], latter[i]))
+        both = jnp.where(
+            is_late,
+            jnp.concatenate([give, keep], axis=0),
+            jnp.concatenate([keep, give], axis=0),
+        )
+        return lax.all_gather(both, ("dp", "seq"), axis=0, tiled=True)
+
+    rim = tokens[:, half - HALO :]
+    halo = jnp.where(is_late, rotated_to(rim, 1, False), rotated_to(rim, 1, True))
+    return gathered(0), gathered(1), swapped(tokens), swapped(cotangent), halo
+
+
+def settled_apart(dims, info, pads, tokens, cotangent, gain, dn, branch, grads, sums, shard):
+    heads, head_dim, state, _ = dims
+    width = heads * head_dim
+    conv_width = width + 4 * state
+    rows, half, model = tokens.shape
+    core = lax.axis_index("dir")
+    is_late = core == 1
+    sum_conv_w, sum_conv_b, gate_sum, skip_sum, small = sums
+
+    def reduced(grad):
+        return lax.psum_scatter(grad, ("dp", "seq"), scatter_dimension=0, tiled=True)
+
+    def halves(values, first_row):
+        keep = lax.dynamic_slice_in_dim(values, first_row + core * half, half, axis=1)
+        give = lax.dynamic_slice_in_dim(values, first_row + (1 - core) * half, half, axis=1)
+        return keep, swapped(give)
+
+    dn_own, dn_other = halves(dn, HALO)
+    branch_own, branch_other = halves(branch, 0)
+    edge = dn[:, :HALO]
+    rim_a, rim_b = rotated_to(edge, -1, False), rotated_to(edge, -1, True)
+    mixed, tokens_grad, gain_sum = run(
+        functools.partial(finish, dims),
+        (rows,),
+        [
+            (info, SMEM), (pads, SMEM), (tokens, by_row(half, model)),
+            (cotangent, by_row(half, model)), (gain, whole(1, model)),
+            (dn_own, by_row(half, model)), (dn_other, by_row(half, model)),
+            (rim_a, by_row(HALO, model)), (rim_b, by_row(HALO, model)),
+            (branch_own, by_row(half, model)), (branch_other, by_row(half, model)),
+        ],
+        [
+            (shape_of(BF, rows, half, model), by_row(half, model)),
+            (shape_of(BF, rows, half, model), by_row(half, model)),
+            (shape_of(F32, 1, model), whole(1, model)),
+        ],
+        [pltpu.VMEM((half, model), F32)],
+        name="finish",
+    )
+
+    def placed(values):
+        empty = jnp.zeros_like(values)
+        return jnp.where(
+            is_late,
+            jnp.concatenate([empty, values], axis=-1),
+            jnp.concatenate([values, empty], axis=-1),
+        )
+
+    def returned(grad):
+        value = reduced(grad)
+        own = lax.dynamic_slice_in_dim(value, core * shard, shard, axis=0)
+        give = lax.dynamic_slice_in_dim(value, (1 - core) * shard, shard, axis=0)
+        other = swapped(give)
+        own, other = own.astype(F32), other.astype(F32)
+        return jnp.where(is_late, other, own), jnp.where(is_late, own, other)
+
+    small_both = placed(small[:2]).reshape(2, 2, LANES)
+    sum_norm, all_conv_w, all_conv_b, small_all, skip_all, gate_all = lax.psum(
+        (
+            gain_sum,
+            jnp.concatenate([placed(sum_conv_w[:, :width]), sum_conv_w[:, width:]], axis=1),
+            jnp.concatenate([placed(sum_conv_b[:, :width]), sum_conv_b[:, width:]], axis=1),
+            jnp.swapaxes(small_both, 0, 1).reshape(4, LANES),
+            placed(skip_sum),
+            placed(gate_sum),
+        ),
+        ("dp", "seq", "dir"),
+    )
+    (pre_a, pre_b), (gate_a, gate_b), (out_a, out_b) = (returned(grad) for grad in grads)
+    owned_out = jnp.concatenate([out_a, out_b], axis=1)
+    owned_in = jnp.concatenate(
+        [
+            gate_a, gate_b, pre_a[:, :width], pre_b[:, :width],
+            pre_a[:, width:conv_width] + pre_b[:, width:conv_width],
+        ],
+        axis=1,
+    )
+    dt_both = jnp.stack([pre_a[:, conv_width:], pre_b[:, conv_width:]])
+    return (
+        mixed, tokens_grad, owned_in, dt_both, owned_out, all_conv_w, all_conv_b, gate_all, skip_all,
+        small_all, sum_norm,
+    )
 
 
 def shards(tokens, starts, pad_len, norm_gain, w_in, w_dt, conv_w, conv_b, dt_bias, a_log, skip,
@@ -638,46 +1204,38 @@
     info = jnp.stack([place * span, core, place, jnp.int32(count)]).astype(jnp.int32)[None]
     pads = pad_len[:, None]
     shard = w_in.shape[0]
-    pad_dt = jnp.zeros((shard, LANES - 2 * heads), BF)
-
-    def columns(c):
-        return (
-            jnp.concatenate(
-                [
-                    w_in[:, inner_width + c * width : inner_width + (c + 1) * width],
-                    w_in[:, 2 * inner_width :],
-                    w_dt[:, c * heads : (c + 1) * heads],
-                    w_dt[:, all_heads + c * heads : all_heads + (c + 1) * heads],
-                    pad_dt,
-                ],
-                axis=1,
-            ),
-            w_in[:, c * width : (c + 1) * width],
-            w_out[:, c * width : (c + 1) * width],
-        )
-
-    first, latter = columns(0), columns(1)
     is_late = core == 1
-
-    def both(own, other):
-        return jnp.where(
-            is_late,
-            jnp.concatenate([other, own], axis=0),
-            jnp.concatenate([own, other], axis=0),
-        )
-
-    def gathered(i):
-        keep = jnp.where(is_late, latter[i], first[i])
-        give = jnp.where(is_late, first[i], latter[i])
-        return lax.all_gather(both(keep, swapped(give)), ("dp", "seq"), axis=0, tiled=True)
-
-    w_pre = gathered(0)
-    w_gate = gathered(1)
-    w_out_c = gathered(2)
-    tokens_other = swapped(tokens)
-    cot_other = swapped(cotangent)
-    rim = tokens[:, half - HALO :]
-    halo = jnp.where(is_late, rotated_to(rim, 1, False), rotated_to(rim, 1, True))
+    direct = lax.axis_size("dp") == 4 and 2 * shard % 16 == 0
+    if direct:
+        chips = 4 * count
+        block = (2 * shard, pre_width), (2 * shard, 2 * width)
+        slab_pre, slab_late, tokens_other, cot_other, halo = run(
+            functools.partial(gather_all, dims, count, (pre_width // 256 * 128 + 128, width)),
+            (),
+            [(w_in, VMEM), (w_dt, VMEM), (w_out, VMEM), (tokens, ANY), (cotangent, ANY)],
+            [
+                (shape_of(BF, chips, *block[0]), ANY), (shape_of(BF, chips, *block[1]), ANY),
+                (shape_of(BF, *tokens.shape), ANY), (shape_of(BF, *tokens.shape), ANY),
+                (shape_of(BF, rows, HALO, model), ANY),
+            ],
+            [
+                pltpu.VMEM((shard, pre_width), BF), pltpu.VMEM((shard, 2 * width), BF),
+                pltpu.VMEM((shard, pre_width), BF), pltpu.VMEM((shard, 2 * width), BF),
+                pltpu.VMEM((shard, pre_width), F32), pltpu.VMEM((shard, 2 * width), F32),
+                pltpu.VMEM(block[0], BF), pltpu.VMEM(block[1], BF),
+                pltpu.SemaphoreType.DMA((gather_copies(count),)),
+                pltpu.SemaphoreType.DMA((gather_copies(count),)),
+                pltpu.SemaphoreType.DMA((2,)),
+            ],
+            name="gather",
+            collective_id=0,
+        )
+        w_pre = slab_pre.reshape(model, pre_width)
+        w_late = slab_late.reshape(model, 2 * width)
+    else:
+        w_pre, w_late, tokens_other, cot_other, halo = gathered_apart(
+            w_in, w_dt, w_out, tokens, cotangent, heads, width, inner_width, is_late
+        )
 
     def mine(vector, size):
         return lax.dynamic_slice_in_dim(vector, core * size, size, axis=-1)
@@ -721,6 +1279,8 @@
         name="front",
     )
     received = around(send)
+    left_half = pl.BlockSpec((model, width), lambda *_: (0, 0))
+    right_half = pl.BlockSpec((model, width), lambda *_: (0, 1))
     at_block = lambda *shape: pl.BlockSpec((1,) + shape, lambda r, b: (r, b) + (0,) * (len(shape) - 1))
     at_second = lambda *shape: pl.BlockSpec((1, shape[0]) + shape[1:], lambda r, b: (r, 0, b, 0))
     block_tab = lambda i: pl.BlockSpec((1, 1, BLOCK, LANES), lambda r, b: (r, i, b, 0))
@@ -748,7 +1308,7 @@
             (y_inner, by_row(2, span, width)), (normed, by_row(ext, model)),
             (cotangent, by_row(half, model)), (cot_other, by_row(half, model)),
             (skip_c, whole(1, width)), (gate_gain_c, whole(1, width)),
-            (w_gate, whole(model, width)), (w_out_c, whole(model, width)),
+            (w_late, left_half), (w_late, right_half),
         ],
         [
             (shape_of(F32, rows, 2, span, width), by_row(2, span, width)),
@@ -774,14 +1334,14 @@
             (d_gated, by_row(span, width)), (d_out, by_row(span, model)),
             (normed, by_row(ext, model)), (decay, by_row(blocks, 2, 8, width)),
             (skip_c, whole(1, width)), (gate_gain_c, whole(1, width)),
-            (w_out_c, whole(model, width)),
+            (w_late, right_half),
         ],
         [
             (shape_of(BF, rows, span, width), by_row(span, width)),
             (shape_of(BF, rows, span, width), by_row(span, width)),
             (shape_of(F32, rows, blocks, 2, state, width), by_row(blocks, 2, state, width)),
             (shape_of(BF, 2, rows, state + CARRY, width), second(2, state + CARRY, width)),
-            (shape_of(F32, rows, span, model), by_row(span, model)),
+            (shape_of(BF, rows, span, model), by_row(span, model)),
             (shape_of(BF, model, width), whole(model, width)),
             (shape_of(BF, model, width), whole(model, width)),
             (shape_of(F32, 1, width), whole(1, width)),
@@ -793,11 +1353,6 @@
     )
     back_received = around(back_send[::-1])
 
-    def reduced(grad):
-        return lax.psum_scatter(grad, ("dp", "seq"), scatter_dimension=0, tiled=True)
-
-    shard_out = reduced(grad_out)
-    shard_gate = reduced(grad_gate)
     dv, dbc, along = run(
         functools.partial(inner_back, dims),
         (rows, blocks),
@@ -830,11 +1385,11 @@
             (normed, by_row(ext, model)), (dz, by_row(span, width)),
             (skip_c, whole(1, width)), (a_log_c, whole(1, LANES)),
             (conv_w_c, whole(conv_len, conv_width)), (w_pre, whole(model, pre_width)),
-            (w_gate, whole(model, width)),
+            (w_late, left_half),
         ],
         [
             (shape_of(BF, model, pre_width), whole(model, pre_width)),
-            (shape_of(F32, rows, ext, model), by_row(ext, model)),
+            (shape_of(BF, rows, ext, model), by_row(ext, model)),
             (shape_of(F32, conv_len, conv_width), whole(conv_len, conv_width)),
             (shape_of(F32, 1, conv_width), whole(1, conv_width)),
             (shape_of(F32, 8, LANES), whole(8, LANES)),
@@ -847,92 +1402,67 @@
         flops=6 * tokens_all * model * pre_width,
         name="back",
     )
-    shard_pre = reduced(grad_pre)
-
-    def halves(values, first_row):
-        keep = lax.dynamic_slice_in_dim(values, first_row + core * half, half, axis=1)
-        give = lax.dynamic_slice_in_dim(values, first_row + (1 - core) * half, half, axis=1)
-        return keep, swapped(give.astype(BF))
-
-    dn_own, dn_other = halves(dn, HALO)
-    branch_own, branch_other = halves(branch, 0)
-    edge = dn[:, :HALO].astype(BF)
-    rim_a, rim_b = rotated_to(edge, -1, False), rotated_to(edge, -1, True)
-    mixed, tokens_grad, gain_sum = run(
-        functools.partial(finish, dims),
-        (rows,),
-        [
-            (info, SMEM), (pads, SMEM), (tokens, by_row(half, model)),
-            (cotangent, by_row(half, model)), (gain, whole(1, model)),
-            (dn_own, by_row(half, model)), (dn_other, by_row(half, model)),
-            (rim_a, by_row(HALO, model)), (rim_b, by_row(HALO, model)),
-            (branch_own, by_row(half, model)), (branch_other, by_row(half, model)),
-        ],
-        [
-            (shape_of(BF, rows, half, model), by_row(half, model)),
-            (shape_of(BF, rows, half, model), by_row(half, model)),
-            (shape_of(F32, 1, model), whole(1, model)),
-        ],
-        [pltpu.VMEM((half, model), F32)],
-        name="finish",
-    )
-
-    def placed(values, size):
-        empty = jnp.zeros_like(values)
-        return jnp.where(
-            is_late,
-            jnp.concatenate([empty, values], axis=-1),
-            jnp.concatenate([values, empty], axis=-1),
-        )
-
-    def by_heads(values):
-        return placed(jnp.sum(values.reshape(heads, head_dim), axis=-1), heads)
-
-    def by_step(values):
-        return jnp.concatenate([placed(values[:heads], heads), placed(values[heads : 2 * heads], heads)])
-
-    sum_norm, all_conv_w, all_conv_b, sum_bias, sum_alog, sum_skip, sum_gate = lax.psum(
-        (
-            gain_sum[0],
-            jnp.concatenate([placed(sum_conv_w[:, :width], width), sum_conv_w[:, width:]], axis=1),
-            jnp.concatenate([placed(sum_conv_b[0, :width], width), sum_conv_b[0, width:]]),
-            by_step(small[0]),
-            by_step(small[1]),
-            by_heads(skip_sum[0]),
-            placed(gate_sum[0], width),
-        ),
-        ("dp", "seq", "dir"),
-    )
-
-    def returned(value):
-        own = lax.dynamic_slice_in_dim(value, core * shard, shard, axis=0)
-        give = lax.dynamic_slice_in_dim(value, (1 - core) * shard, shard, axis=0)
-        other = swapped(give)
-        own, other = own.astype(F32), other.astype(F32)
-        return jnp.where(is_late, other, own), jnp.where(is_late, own, other)
-
-    out_a, out_b = returned(shard_out)
-    gate_a, gate_b = returned(shard_gate)
-    pre_a, pre_b = returned(shard_pre)
-    owned_out = jnp.concatenate([out_a, out_b], axis=1)
-    owned_in = jnp.concatenate(
-        [
-            gate_a, gate_b, pre_a[:, :width], pre_b[:, :width],
-            pre_a[:, width:conv_width] + pre_b[:, width:conv_width],
-        ],
-        axis=1,
-    )
-    last = conv_width
-    owned_dt = jnp.concatenate(
-        [
-            pre_a[:, last : last + heads], pre_b[:, last : last + heads],
-            pre_a[:, last + heads : last + 2 * heads], pre_b[:, last + heads : last + 2 * heads],
-        ],
-        axis=1,
-    )
+    grads = (grad_pre, grad_gate, grad_out)
+    sums = (sum_conv_w, sum_conv_b, gate_sum, skip_sum, small)
+    if direct:
+        widths = (pre_width, width, width)
+        scratch = []
+        for size in widths:
+            scratch += [
+                pltpu.VMEM((2, count, 2 * shard, size), BF), pltpu.VMEM((count, 2 * shard, size), BF),
+                pltpu.VMEM((count - 1, 2 * shard, size), BF), pltpu.VMEM((count, 2 * shard, size), BF),
+                pltpu.VMEM((count - 1, 2 * shard, size), BF), pltpu.VMEM((2 * shard, size), F32),
+            ]
+        scratch += [pltpu.VMEM((shard, size), F32) for size in widths]
+        lanes = conv_width
+        scratch += [
+            pltpu.VMEM((rows, half, model), BF), pltpu.VMEM((rows, half, model), BF),
+            pltpu.VMEM((2, rows, HALO, model), BF), pltpu.VMEM((half, model), F32),
+            pltpu.VMEM((8, lanes), F32), pltpu.VMEM((2, 8, lanes), F32), pltpu.VMEM((2, 8, lanes), F32),
+            pltpu.VMEM((count - 1, 8, lanes), F32), pltpu.VMEM((8, lanes), F32),
+            pltpu.SemaphoreType.DMA((settle_copies(count),)),
+            pltpu.SemaphoreType.DMA((settle_copies(count) + 1,)),
+        ]
+        (mixed, tokens_grad, owned_in, dt_both, owned_out, all_conv_w, all_conv_b, sum_gate, skip_all,
+         small_all, sum_norm) = run(
+            functools.partial(settle, dims, count, (pre_width // 256 * 128 + 128, width // 2, width // 2)),
+            (),
+            [
+                (pads, SMEM), (tokens, VMEM), (cotangent, VMEM), (gain, VMEM), (dn, VMEM),
+                (branch, VMEM),
+            ]
+            + [
+                (grad.reshape(4 * count, 2 * shard, grad.shape[1]), VMEM) for grad in grads
+            ]
+            + [(value, VMEM) for value in sums],
+            [
+                (shape_of(BF, rows, half, model), VMEM), (shape_of(BF, rows, half, model), VMEM),
+                (shape_of(F32, shard, w_in.shape[1]), VMEM), (shape_of(F32, 2, shard, LANES), VMEM),
+                (shape_of(F32, shard, inner_width), VMEM),
+                (shape_of(F32, conv_len, xbc_width), VMEM), (shape_of(F32, 1, xbc_width), VMEM),
+                (shape_of(F32, 1, inner_width), VMEM), (shape_of(F32, 1, inner_width), VMEM),
+                (shape_of(F32, 4, LANES), VMEM), (shape_of(F32, 1, model), VMEM),
+            ],
+            scratch,
+            name="settle",
+            collective_id=1,
+        )
+    else:
+        (mixed, tokens_grad, owned_in, dt_both, owned_out, all_conv_w, all_conv_b, sum_gate, skip_all,
+         small_all, sum_norm) = settled_apart(
+            dims, info, pads, tokens, cotangent, gain, dn, branch, grads, sums, shard
+        )
+
+    def by_step(first, second):
+        return jnp.concatenate(
+            [first[:heads], second[:heads], first[heads : 2 * heads], second[heads : 2 * heads]]
+        )
+
+    owned_dt = by_step(dt_both[0].T, dt_both[1].T).T
     return (
-        mixed, tokens_grad, sum_norm, owned_in, owned_dt, all_conv_w, all_conv_b, sum_bias,
-        sum_alog, sum_skip, sum_gate, owned_out,
+        mixed, tokens_grad, sum_norm[0], owned_in, owned_dt, all_conv_w, all_conv_b[0],
+        by_step(small_all[0], small_all[2]), by_step(small_all[1], small_all[3]),
+        jnp.sum(skip_all.reshape(all_heads, head_dim), axis=-1), sum_gate[0], owned_out,
     )
 
 

time: 623 us -> 252 us (0.40)
  waiting for transfers between devices: 426 us -> 16.3 us
  Pallas kernels: 87 us -> 196 us
  blocking collectives: 40.8 us -> 0 us
  between operations: 14.5 us -> 0.79 us
  starting transfers between devices: 20.1 us -> 7.85 us
    reduce_scatter x3 -> x0, waiting for transfers between devices: 275 us -> none  [reduced(): lax.psum_scatter(grad, ('dp', 'seq'), scatter_dimension=0, tiled=True)]
    all_gather x3 -> x0, waiting for transfers between devices: 134 us -> none  [gathered(): lax.all_gather(both(keep, swapped(give)), ('dp', 'seq'), axis=0, tiled=True)]
    pallas_call x7 -> x8, Pallas kernels: 87 us -> 196 us  [run(): pl.pallas_call(body, grid=grid, out_shape=[s for s, _ in outs], in_specs=...]
    psum x1 -> x0, blocking collectives: 40.8 us -> none  [shards(): lax.psum((gain_sum[0], jnp.concatenate([placed(sum_conv_w[:, :width], wid...]
    ppermute x4 -> x0, starting transfers between devices: 10.1 us -> none  [rotated_to(): return lax.ppermute(value, ('seq', 'dir'), pairs)]
  transfers between devices with their start and end apart: 27 -> 7, of which waited for: 16 -> 4; matrix products, arithmetic and copies ran while one was open for 4% -> 1% of each run, Pallas kernels for 10% -> 9%
where the time goes in v1:
time: 252 us; the launch traced here: 251 us
  Pallas kernels  196 us (78%)
  local copies, waits for them, and re-layouts  17.2 us (7%)
  waiting for transfers between devices  16.3 us (6%)
  other arithmetic  13.1 us (5%)
  starting transfers between devices  7.85 us (3%)
    pallas_call x8, Pallas kernels, run(): pl.pallas_call(body, grid=grid, out_shape=[s for s, _ in outs], in_specs=...  196 us
    ppermute x6, waiting for transfers between devices, rotated(): lax.ppermute(value, 'seq', [(i, (i + steps) % count) for i in range(count)])  14.5 us
    ppermute x6, starting transfers between devices, rotated(): lax.ppermute(value, 'seq', [(i, (i + steps) % count) for i in range(count)])  7.78 us
    unnamed x17, local copies, waits for them, and re-layouts  6.41 us
  transfers between devices with their start and end apart: 7, of which 4 were waited for; matrix products, arithmetic and copies ran while one was open for 1% of the time, Pallas kernels for 9%

profile of v1, /device:TPU:0, one launch (start us, length us, event | category | flops | bytes accessed | tf_op | source)
XLA Modules:
  0.0 250.7 jit_solution(17264547890012414685)
XLA Ops:
  0.6 0.7 slice.125
  1.3 0.7 slice.124
  2.1 1.3 copy.28.pads
  3.4 0.7 slice.127
  4.1 0.8 fusion.5
  5.0 0.8 fusion.4
  6.0 1.3 broadcast_in_dim.28.gain
  7.3 0.8 dynamic_slice.25
  8.0 0.6 pad_maximum_fusion.3
  8.6 0.6 pad_maximum_fusion.2.conv_w
  9.2 0.7 add_bitcast_fusion.info
  9.9 0.6 fusion.1
  10.5 52.4 %gather.1 = (bf16[16,48,1152]{2,1,0:T(8,128)(2,1)}, bf16[16,48,1536]{2,1,0:T(8,128)(2,1)}, bf16[2,160,768]{2,1,0:T(8,128)(2,1)}, bf16[2,160,768]{2,1,0:T(8,128)(2,1)}, bf16[2,16,768]{2,1,0:T(8,128)(2,1)}) custom-call(bf16[24,3328]{1,0:T(8,128)(2,1)} %w_in.1, bf16[24,48]{1,0:T(8,128)(2,1)} %w_dt.1, bf16[24,1536]{1,0:T(8,128)(2,1)} %w_out.1, ...), custom_call_target="tpu_custom_call" | custom-call | bytes 6379776 | tf_op jit(solution)/shard_map/gather/pallas_call | solution.py:1010
  63.0 12.2 %front.1 = (bf16[2,336,768]{2,1,0:T(8,128)(2,1)}, bf16[2,336,1024]{2,1,0:T(8,128)(2,1)}, bf16[2,320,1024]{2,1,0:T(8,128)(2,1)}, f32[2,320,1024]{2,1,0:T(8,128)},...) custom-call(s32[1,4]{1,0:T(1,128)} %add_bitcast_fusion.info, ...), custom_call_target="tpu_custom_call" | custom-call | flops 1132462080 | bytes 15093816 | tf_op jit(solution)/shard_map/front/pallas_call | solution.py:1010
  75.1 1.1 select_bitcast_fusion.5
  76.3 2.1 collective-permute-start
  78.3 1.8 collective-permute-start.2
  80.3 0.6 broadcast_in_dim.35.gate_gain
  81.0 0.7 broadcast_in_dim_reshape.3.skip
  81.6 7.2 %inner.1.y_in = f32[2,2,320,768]{3,2,1,0:T(8,128)} custom-call(s32[1,4]{1,0:T(1,128)} %add_bitcast_fusion.info, s32[2,4]{1,0:T(2,128)} %starts.9, bf16[2,320,1024]{2,1,0:T(8,128)(2,1)} %get-tuple-element.67.xbc, f32[2,5,320,128]{3,2,1,0:T(8,128)} %get-tuple-element.68.tab, f32[2,2,24,160]{3,2,1,0:T(8,128)} %get-tuple-element.69.cumt, ...), custom_call_target="tpu_custom_call" | custom-call | flops 629145600 | bytes 8908848 | tf_op jit(solution)/shard_map/inner/pallas_call | solution.py:1010
  88.8 0.5 collective-permute-done.2
  89.3 9.2 %collective-permute-done.1 = bf16[2,80,768]{2,1,0:T(8,128)(2,1)S(1)} collective-permute-done((bf16[2,80,768]{2,1,0:T(8,128)(2,1)S(1)}, bf16[2,80,768]{2,1,0:T(8,128)(2,1)S(1)}, u32[]{:S(2)}, u32[]{:S(2)}) %collective-permute-start.1) | collective-permute-done | bytes 245792 | tf_op jit(solution)/shard_map/ppermute | solution.py:1040
  98.5 0.9 pad_maximum_fusion.received
  99.4 9.0 %outer.1 = (f32[2,2,320,768]{3,2,1,0:T(8,128)}, f32[2,2,2,64,768]{4,3,2,1,0:T(8,128)}, f32[2,320,128]{2,1,0:T(8,128)}, f32[2,320,768]{2,1,0:T(8,128)}, f32[2,320...) custom-call(s32[1,4]{1,0:T(1,128)} %add_bitcast_fusion.info, s32[2,4]{1,0:T(2,128)} %starts.9, s32[2,1]{1,0:T(2,128)} %copy.28.pads, ...), custom_call_target="tpu_custom_call" | custom-call | flops 1509949440 | bytes 26875960 | tf_op jit(solution)/shard_map/outer/pallas_call | solution.py:1010
  108.5 1.8 collective-permute-done.3.others
  110.4 0.7 copy-done
  111.1 15.1 %turn.1 = (bf16[2,320,768]{2,1,0:T(8,128)(2,1)}, bf16[2,320,768]{2,1,0:T(8,128)(2,1)}, f32[2,2,2,64,768]{4,3,2,1,0:T(8,128)}, bf16[2,2,80,768]{3,2,1,0:T(8,128)(...) custom-call(f32[2,320,128]{2,1,0:T(8,128)} %get-tuple-element.74.sum, ...), custom_call_target="tpu_custom_call" | custom-call | flops 2264924160 | bytes 23425024 | tf_op jit(solution)/shard_map/turn/pallas_call | solution.py:1010
  126.2 1.1 select_bitcast_fusion.2
  127.4 3.8 %collective-permute-start.6 = (bf16[2,80,768]{2,1,0:T(8,128)(2,1)S(1)}, bf16[2,80,768]{2,1,0:T(8,128)(2,1)S(1)}, u32[]{:S(2)}, u32[]{:S(2)}) collective-permute-start(bf16[2,80,768]{2,1,0:T(8,128)(2,1)S(1)} %get-tuple-element.111), channel_id=1, source_target_pairs={{0,6},{2,0},{4,2},{6,4},{1,7},{3,1},{5,3},{7,5},{8,14},{10,8},{12,... | collective-permute-start | bytes 737288 | tf_op jit(solution)/shard_map/ppermute | solution.py:1040
  131.2 15.5 %inner_back.1 = (f32[2,2,320,768]{3,2,1,0:T(8,128)}, f32[2,320,256]{2,1,0:T(8,128)}, f32[2,320,128]{2,1,0:T(8,128)}) custom-call(s32[1,4]{1,0:T(1,128)} %add_bitcast_fusion.info, s32[2,4]{1,0:T(2,128)} %starts.9, bf16[2,320,1024]{2,1,0:T(8,128)(2,1)} %get-tuple-element.67.xbc, f32[2,5,320,128]{3,2,1,0:T(8,128)} %get-tuple-element.68.tab, ...), custom_call_target="tpu_custom_call" | custom-call | flops 1258291200 | bytes 16379952 | tf_op jit(solution)/shard_map/inner_back/pallas_call | solution.py:1010
  146.7 4.8 %collective-permute-done.5 = bf16[2,80,768]{2,1,0:T(8,128)(2,1)S(1)} collective-permute-done((bf16[2,80,768]{2,1,0:T(8,128)(2,1)S(1)}, bf16[2,80,768]{2,1,0:T(8,128)(2,1)S(1)}, u32[]{:S(2)}, u32[]{:S(2)}) %collective-permute-start.5) | collective-permute-done | bytes 245792 | tf_op jit(solution)/shard_map/ppermute | solution.py:1040
  151.5 1.0 pad_maximum_fusion.1.received
  152.5 24.1 %back.1 = (bf16[768,1152]{1,0:T(8,128)(2,1)}, bf16[2,336,768]{2,1,0:T(8,128)(2,1)}, f32[4,1024]{1,0:T(4,128)}, f32[1,1024]{1,0:T(1,128)}, f32[8,128]{1,0:T(8,128)}) custom-call(s32[1,4]{1,0:T(1,128)} %add_bitcast_fusion.info, s32[2,4]{1,0:T(2,128)} %starts.9, bf16[3,2,80,768]{3,2,1,0:T(8,128)(2,1)} %pad_maximum_fusion.1.received, ...), custom_call_target="tpu_custom_call" | custom-call | flops 3397386240 | bytes 27881008 | tf_op jit(solution)/shard_map/back/pallas_call | solution.py:1010
  176.5 60.0 %settle.1 = (bf16[2,160,768]{2,1,0:T(8,128)(2,1)}, bf16[2,160,768]{2,1,0:T(8,128)(2,1)}, f32[24,3328]{1,0:T(8,128)}, f32[2,24,128]{2,1,0:T(8,128)}, f32[24,1536]...) custom-call(s32[2,1]{1,0:T(2,128)} %copy.28.pads, ...), custom_call_target="tpu_custom_call" | custom-call | bytes 8688648 | tf_op jit(solution)/shard_map/settle/pallas_call | solution.py:1010
  236.6 1.0 slice_bitcast_fusion.5
  237.6 1.3 reduce
  238.9 1.3 reduce.1
  240.2 0.7 reduce.2
  240.9 1.3 reduce.3
  242.3 0.6 reduce_sum.9
  242.9 0.7 slice_bitcast_fusion.1
  243.7 0.7 maximum_bitcast_fusion
  244.4 0.6 pad_maximum_fusion.6
  245.0 1.8 copy.34
  246.9 1.8 copy.35
  248.7 0.7 copy.36
  249.4 0.6 copy.37
  250.0 0.7 copy.38
  (29 shorter events, 0.9 us)
Async XLA Ops:
  62.9 17.2 %copy-start.5 = (f32[24]{0:T(128)S(1)}, f32[24]{0:T(128)}, u32[]{:S(2)}) copy-start(f32[24]{0:T(128)} %param.24) | copy-start | bytes 292
  62.9 17.3 %copy-start.4 = (f32[1536]{0:T(1024)S(1)}, f32[1536]{0:T(1024)}, u32[]{:S(2)}) copy-start(f32[1536]{0:T(1024)} %param.25) | copy-start | bytes 18436
  76.3 12.6 %collective-permute-start = (bf16[2,80,768]{2,1,0:T(8,128)(2,1)S(1)}, bf16[2,80,768]{2,1,0:T(8,128)(2,1)S(1)}, u32[]{:S(2)}, u32[]{:S(2)}) collective-permute-start(bf16[2,80,768]{2,1,0:T(8,128)(2,1)S(1)} %get-tuple-element.113), channel_id=1, source_target_pairs={{0,2},{2,4},{4,6},{6,0},{1,3},{3,5},{5,7},{7,1},{8,10},{10,12},{12... | collective-permute-start | bytes 737288 | tf_op jit(solution)/shard_map/ppermute | solution.py:1040
  78.3 11.0 %collective-permute-start.2 = (bf16[2,80,768]{2,1,0:T(8,128)(2,1)S(1)}, bf16[2,80,768]{2,1,0:T(8,128)(2,1)S(1)}, u32[]{:S(2)}, u32[]{:S(2)}) collective-permute-start(bf16[2,80,768]{2,1,0:T(8,128)(2,1)S(1)} %get-tuple-element.114), channel_id=1, source_target_pairs={{0,6},{2,0},{4,2},{6,4},{1,7},{3,1},{5,3},{7,5},{8,14},{10,8},{12,... | collective-permute-start | bytes 737288 | tf_op jit(solution)/shard_map/ppermute | solution.py:1040
  80.1 18.4 %collective-permute-start.1 = (bf16[2,80,768]{2,1,0:T(8,128)(2,1)S(1)}, bf16[2,80,768]{2,1,0:T(8,128)(2,1)S(1)}, u32[]{:S(2)}, u32[]{:S(2)}) collective-permute-start(bf16[2,80,768]{2,1,0:T(8,128)(2,1)S(1)} %get-tuple-element.115), channel_id=1, source_target_pairs={{0,4},{2,6},{4,0},{6,2},{1,5},{3,7},{5,1},{7,3},{8,12},{10,14},{12... | collective-permute-start | bytes 737288 | tf_op jit(solution)/shard_map/ppermute | solution.py:1040
  108.5 1.9 collective-permute-start.3
  110.4 0.7 copy-start
  127.3 19.4 %collective-permute-start.4 = (bf16[2,80,768]{2,1,0:T(8,128)(2,1)S(1)}, bf16[2,80,768]{2,1,0:T(8,128)(2,1)S(1)}, u32[]{:S(2)}, u32[]{:S(2)}) collective-permute-start(bf16[2,80,768]{2,1,0:T(8,128)(2,1)S(1)} %get-tuple-element.110), channel_id=1, source_target_pairs={{0,2},{2,4},{4,6},{6,0},{1,3},{3,5},{5,7},{7,1},{8,10},{10,12},{12... | collective-permute-start | bytes 737288 | tf_op jit(solution)/shard_map/ppermute | solution.py:1040
  127.4 19.3 %collective-permute-start.6 = (bf16[2,80,768]{2,1,0:T(8,128)(2,1)S(1)}, bf16[2,80,768]{2,1,0:T(8,128)(2,1)S(1)}, u32[]{:S(2)}, u32[]{:S(2)}) collective-permute-start(bf16[2,80,768]{2,1,0:T(8,128)(2,1)S(1)} %get-tuple-element.111), channel_id=1, source_target_pairs={{0,6},{2,0},{4,2},{6,4},{1,7},{3,1},{5,3},{7,5},{8,14},{10,8},{12,... | collective-permute-start | bytes 737288 | tf_op jit(solution)/shard_map/ppermute | solution.py:1040
  131.2 20.3 %collective-permute-start.5 = (bf16[2,80,768]{2,1,0:T(8,128)(2,1)S(1)}, bf16[2,80,768]{2,1,0:T(8,128)(2,1)S(1)}, u32[]{:S(2)}, u32[]{:S(2)}) collective-permute-start(bf16[2,80,768]{2,1,0:T(8,128)(2,1)S(1)} %get-tuple-element.112), channel_id=1, source_target_pairs={{0,4},{2,6},{4,0},{6,2},{1,5},{3,7},{5,1},{7,3},{8,12},{10,14},{12... | collective-permute-start | bytes 737288 | tf_op jit(solution)/shard_map/ppermute | solution.py:1040
  236.5 12.2 %copy-start.1 = (f32[24,3328]{1,0:T(8,128)S(1)}, f32[24,3328]{1,0:T(8,128)}, u32[]{:S(2)}) copy-start(f32[24,3328]{1,0:T(8,128)} %get-tuple-element.155) | copy-start | bytes 958468
  236.6 12.9 %copy-start.3 = (f32[4,1792]{1,0:T(4,128)S(1)}, f32[4,1792]{1,0:T(4,128)}, u32[]{:S(2)}) copy-start(f32[4,1792]{1,0:T(4,128)} %get-tuple-element.157) | copy-start | bytes 86020
  236.6 13.5 %copy-start.2 = (f32[24,1536]{1,0:T(8,128)S(1)}, f32[24,1536]{1,0:T(8,128)}, u32[]{:S(2)}) copy-start(f32[24,1536]{1,0:T(8,128)} %get-tuple-element.163) | copy-start | bytes 442372
